TPU v7x, 128 devices: a whole 4x4x4 slice. The times are simulated.
128 devices in a mesh: section: 2 (over core), seq: 4 (over x), fsdp: 16 (over z, y).
Axes of the slice: x: 4, y: 4, z: 4, core: 2. Of those that a mesh axis runs over, the one named last changes fastest.
Arguments:
- block_in: bfloat16 [2, 16, 256, 1024], P(None, 'fsdp', 'seq'), may hold values from -6 to 6
- cotangent: bfloat16 [2, 16, 256, 1024], P(None, 'fsdp', 'seq'), may hold values from -6 to 6
- perm_rows: int32 [2, 16, 256], P(None, 'fsdp'), may hold values from 0 to 255, each once within a row
- doc_lengths: int32 [2, 16, 4], P(None, 'fsdp'), may hold values from 1 to 192, 256 in all within a row
- norm_in: float32 [2, 1024], P('section'), may hold values from 0.5 to 1.5
- w_qkv: bfloat16 [2, 1024, 3072], P('section', 'fsdp'), may hold values from -0.1875 to 0.1875
- w_beta: bfloat16 [2, 1024, 8], P('section', 'fsdp'), may hold values from -0.1875 to 0.1875
- conv_w: float32 [2, 4, 3, 1024], P('section'), may hold values from -3 to 3
- norm_head: float32 [2, 128], P('section'), may hold values from 0.5 to 1.5
- w_out: bfloat16 [2, 1024, 1024], P('section', 'fsdp'), may hold values from -0.1875 to 0.1875
- norm_ffn: float32 [2, 1024], P('section'), may hold values from 0.5 to 1.5
- w_ffn: bfloat16 [2, 2, 1024, 2816], P('section', None, None, 'fsdp'), may hold values from -0.1875 to 0.1875
- w_down: bfloat16 [2, 2816, 1024], P('section', 'fsdp'), may hold values from -0.109375 to 0.109375
Outputs:
- block_out: bfloat16 [2, 16, 256, 1024], P(None, 'fsdp', 'seq')
- input_grad: bfloat16 [2, 16, 256, 1024], P(None, 'fsdp', 'seq')
- grad_norm_in: float32 [2, 1024], P('section')
- grad_qkv: float32 [2, 1024, 3072], P('section', 'fsdp')
- grad_beta: float32 [2, 1024, 8], P('section', 'fsdp')
- grad_conv: float32 [2, 4, 3, 1024], P('section')
- grad_norm_head: float32 [2, 128], P('section')
- grad_out: float32 [2, 1024, 1024], P('section', 'fsdp')
- grad_norm_ffn: float32 [2, 1024], P('section')
- grad_ffn: float32 [2, 2, 1024, 2816], P('section', None, None, 'fsdp')
- grad_down: float32 [2, 2816, 1024], P('section', 'fsdp')
Inputs may be any that keep to these rules, and one draw needn't show every extreme that they name: `perm_rows`: each pack's row is a permutation of its positions. `doc_lengths`: A pack's lengths sum to 256; its longest document has exactly 192 tokens.
All inputs are finite; a program needn't handle non-finite values.
Results may differ from a plain program's by a relative error of at most 0.029.
Values may be sent and summed in bfloat16 or wider, within the bound.
A program may use at most 192 MiB of HBM per device.

v0:
```python
from functools import partial

import jax
import jax.numpy as jnp
from jax import lax
from jax.sharding import PartitionSpec as P

D = 1024
H = 8
HD = 128
SPAN = 64


def swapped(block, axis, distance):
    count = lax.axis_size(axis)
    route = []
    for low in range(count):
        high = low | 1 << distance
        if high != low and high < count:
            route += [(low, high), (high, low)]
    return lax.ppermute(block, axis, route)


def exact_einsum(form, left_side, right_side):
    return jnp.einsum(form, left_side, right_side, precision=lax.Precision.HIGHEST)


def pass_section(message):
    return swapped(message, "section", 0)


def rms_scale(values):
    return lax.rsqrt(jnp.mean(values * values, axis=-1, keepdims=True) + 1e-06)


def rms_back(grad_normed, values, scale_rows, scale_by):
    weighted = grad_normed * scale_by
    inner = jnp.mean(weighted * values, axis=-1, keepdims=True)
    grad_values = scale_rows * weighted - values * (scale_rows * scale_rows * scale_rows) * inner
    return (grad_values, jnp.sum(grad_normed * values * scale_rows, axis=0))


def unit_rows(values):
    return values * lax.rsqrt(jnp.sum(values * values, axis=-1, keepdims=True) + 1e-06)


def doc_index(doc_len, row_count):
    places = jnp.arange(row_count, dtype=jnp.int32)
    doc_ends = jnp.cumsum(doc_len)
    return jnp.sum((places[:, None] >= doc_ends[None, :]).astype(jnp.int32), axis=1)


def short_conv(series, kernel, doc_ids):
    row_count = series.shape[0]
    spread = (1,) * (series.ndim - 1)
    combined = series * kernel[0]
    for lag_step in range(1, kernel.shape[0]):
        padding = ((lag_step, 0),) + ((0, 0),) * (series.ndim - 1)
        shifted = jnp.pad(series, padding)[:row_count]
        earlier = jnp.pad(doc_ids, (lag_step, 0), constant_values=-1)[:row_count]
        within = (earlier == doc_ids).astype(series.dtype).reshape((row_count,) + spread)
        combined = combined + shifted * kernel[lag_step] * within
    return combined


def delta_blocks(queries, key_rows, values, strengths, doc_ids):
    row_count, head_count, head_width = queries.shape
    block_count = row_count // SPAN

    def to_blocks(array):
        return jnp.swapaxes(array.reshape((block_count, SPAN) + array.shape[1:]), 1, 2)

    query_blocks = to_blocks(queries)
    key_blocks = to_blocks(key_rows)
    value_blocks = to_blocks(values)
    strength_blocks = to_blocks(strengths)
    doc_blocks = doc_ids.reshape(block_count, SPAN)
    same_doc = (doc_blocks[:, :, None] == doc_blocks[:, None, :]).astype(jnp.float32)
    strict_lower = jnp.tril(jnp.ones((SPAN, SPAN), jnp.float32), -1)
    with_diagonal = jnp.tril(jnp.ones((SPAN, SPAN), jnp.float32))
    key_gram = exact_einsum("nhid,nhjd->nhij", key_blocks, key_blocks)
    system = (
        jnp.eye(SPAN, dtype=jnp.float32)
        + strength_blocks[..., :, None] * key_gram * (strict_lower * same_doc)[:, None]
    )
    sources = strength_blocks[..., None] * jnp.concatenate([key_blocks, value_blocks], axis=-1)
    solved = lax.linalg.triangular_solve(
        system, sources, left_side=True, lower=True, unit_diagonal=True
    )
    key_mix = solved[..., :head_width]
    value_mix = solved[..., head_width:]
    scores = (
        exact_einsum("nhid,nhjd->nhij", query_blocks, key_blocks)
        * (with_diagonal * same_doc)[:, None]
    )
    prior_last = jnp.concatenate([jnp.full((1,), -1, jnp.int32), doc_blocks[:-1, -1]])
    carried = (doc_blocks == prior_last[:, None]).astype(jnp.float32)
    closing = (doc_blocks == doc_blocks[:, -1:]).astype(jnp.float32)

    def advance(memory, pieces):
        (
            block_query,
            block_key,
            block_keymix,
            block_valmix,
            block_scores,
            block_carried,
            block_closing,
        ) = pieces
        carried_col = block_carried[None, :, None]
        fresh = block_valmix - carried_col * exact_einsum("hcd,hvd->hcv", block_keymix, memory)
        produced = carried_col * exact_einsum("hcd,hvd->hcv", block_query, memory) + exact_einsum(
            "hij,hjv->hiv", block_scores, fresh
        )
        memory = block_carried[-1] * memory + exact_einsum(
            "hcv,hcd->hvd", fresh * block_closing[None, :, None], block_key
        )
        return (memory, produced)

    start_memory = jnp.zeros((head_count, head_width, head_width), jnp.float32)
    _, produced = lax.scan(
        advance,
        start_memory,
        (query_blocks, key_blocks, key_mix, value_mix, scores, carried, closing),
    )
    return jnp.swapaxes(produced, 1, 2).reshape(row_count, head_count, head_width)


def mixer_local(projected, logits, kernel, head_gain, perm_row, doc_len):
    row_count, _, head_count, head_width = projected.shape
    places = jnp.arange(row_count, dtype=jnp.int32)
    inverse = jnp.zeros((row_count,), jnp.int32).at[perm_row].set(places)
    series = projected[inverse]
    strengths = jax.nn.sigmoid(logits[inverse][:, 0])
    doc_ids = doc_index(doc_len, row_count)
    activated = jax.nn.silu(
        short_conv(series, kernel.reshape(kernel.shape[0], 3, head_count, head_width), doc_ids)
    )
    queries = unit_rows(activated[:, 0]) * head_width ** (-0.5)
    key_rows = unit_rows(activated[:, 1])
    values = activated[:, 2]
    produced = delta_blocks(queries, key_rows, values, strengths, doc_ids)
    normed = (
        produced
        * lax.rsqrt(jnp.mean(produced * produced, axis=-1, keepdims=True) + 1e-05)
        * head_gain
    )
    return normed[perm_row]


def local(
    block_in,
    cotangent,
    perm_rows,
    doc_lengths,
    norm_in,
    w_qkv,
    w_beta,
    conv_w,
    norm_head,
    w_out,
    norm_ffn,
    w_ffn,
    w_down,
):
    micro = block_in.shape[0]
    tok_rows = block_in.shape[2]
    seq_count = lax.axis_size("seq")
    heads_here = H // seq_count
    section_first = lax.axis_index("section") == 0
    gain_in = norm_in[0]
    gain_ffn = norm_ffn[0]
    head_gain = norm_head[0]
    head_start = lax.axis_index("seq") * (heads_here * HD)
    kernel = lax.dynamic_slice_in_dim(conv_w[0], head_start, heads_here * HD, 2)
    full_qkv, full_beta, full_out = (
        lax.all_gather(w_qkv[0], "fsdp", axis=0, tiled=True),
        lax.all_gather(w_beta[0], "fsdp", axis=0, tiled=True),
        lax.all_gather(w_out[0], "fsdp", axis=0, tiled=True),
    )
    stacked = jnp.concatenate([w_ffn[0], jnp.swapaxes(w_down[0], 0, 1)[None]], axis=0)
    full_ffn = lax.all_gather(stacked, "fsdp", axis=2, tiled=True)
    gate_weight, up_weight, down_weight = (full_ffn[0], full_ffn[1], full_ffn[2])
    received = jnp.zeros((tok_rows, D), jnp.bfloat16)
    caches = []
    block_rows = []
    for tick_index in range(micro + 1):
        own_rows = block_in[tick_index, 0] if tick_index < micro else jnp.zeros_like(received)
        rows_in = jnp.where(section_first, own_rows, received).astype(jnp.float32)
        early = min(tick_index, micro - 1)
        later = max(tick_index - 1, 0)
        perm_row = jnp.where(section_first, perm_rows[early, 0], perm_rows[later, 0])
        doc_len = jnp.where(section_first, doc_lengths[early, 0], doc_lengths[later, 0])
        scale_in = rms_scale(rows_in)
        normed_in = (rows_in * scale_in * gain_in).astype(jnp.bfloat16)
        projected = jnp.dot(normed_in, full_qkv, preferred_element_type=jnp.float32).astype(
            jnp.bfloat16
        )
        logits = jnp.dot(normed_in, full_beta, preferred_element_type=jnp.float32).astype(
            jnp.bfloat16
        )
        head_proj, head_logits = (
            lax.all_to_all(
                projected.reshape(tok_rows, 3, H, HD),
                "seq",
                split_axis=2,
                concat_axis=0,
                tiled=True,
            ),
            lax.all_to_all(
                logits.reshape(tok_rows, 1, H), "seq", split_axis=2, concat_axis=0, tiled=True
            ),
        )
        mixer_fn = partial(mixer_local, perm_row=perm_row, doc_len=doc_len)
        mixed_out, mixer_back = jax.vjp(
            mixer_fn,
            head_proj.astype(jnp.float32),
            head_logits.astype(jnp.float32),
            kernel,
            head_gain,
        )
        attended = lax.all_to_all(
            mixed_out.astype(jnp.bfloat16), "seq", split_axis=0, concat_axis=1, tiled=True
        ).reshape(tok_rows, D)
        residual = rows_in + jnp.dot(attended, full_out, preferred_element_type=jnp.float32)
        scale_ffn = rms_scale(residual)
        normed_ffn = (residual * scale_ffn * gain_ffn).astype(jnp.bfloat16)
        ffn_rows = normed_ffn
        gate_pre = jnp.dot(ffn_rows, gate_weight, preferred_element_type=jnp.float32)
        up_pre = jnp.dot(ffn_rows, up_weight, preferred_element_type=jnp.float32)
        hidden = (jax.nn.silu(gate_pre) * up_pre).astype(jnp.bfloat16)
        update = jnp.einsum("tf,df->td", hidden, down_weight, preferred_element_type=jnp.float32)
        result = (residual + update).astype(jnp.bfloat16)
        received = pass_section(result)
        if tick_index >= 1:
            block_rows.append(jnp.where(section_first, received, result))
        caches.append(
            (
                rows_in,
                scale_in,
                normed_in,
                mixer_back,
                attended,
                residual,
                scale_ffn,
                ffn_rows,
                gate_pre,
                up_pre,
                hidden,
            )
        )
    returned = jnp.zeros((tok_rows, D), jnp.bfloat16)
    grad_rows = [None] * micro
    kept = [None] * (micro + 1)
    kernel_acc = jnp.zeros(kernel.shape, jnp.float32)
    gain_in_acc = jnp.zeros((D,), jnp.float32)
    gain_ffn_acc = jnp.zeros((D,), jnp.float32)
    head_gain_acc = jnp.zeros((HD,), jnp.float32)
    for turn_index in range(micro + 1):
        slot_index = micro - turn_index
        (
            rows_in,
            scale_in,
            normed_in,
            mixer_back,
            attended,
            residual,
            scale_ffn,
            ffn_rows,
            gate_pre,
            up_pre,
            hidden,
        ) = caches[slot_index]
        given = cotangent[slot_index - 1, 0] if slot_index >= 1 else jnp.zeros_like(returned)
        grad_outer = jnp.where(section_first, returned, given).astype(jnp.float32)
        grad_low = grad_outer.astype(jnp.bfloat16)
        grad_hidden = jnp.dot(grad_low, down_weight, preferred_element_type=jnp.float32)
        gate_sig = jax.nn.sigmoid(gate_pre)
        grad_gate = (grad_hidden * up_pre * gate_sig * (1.0 + gate_pre * (1.0 - gate_sig))).astype(
            jnp.bfloat16
        )
        grad_up = (grad_hidden * gate_pre * gate_sig).astype(jnp.bfloat16)
        grad_normed_ffn = jnp.einsum(
            "tf,df->td", grad_gate, gate_weight, preferred_element_type=jnp.float32
        ) + jnp.einsum("tf,df->td", grad_up, up_weight, preferred_element_type=jnp.float32)
        grad_resid_part, gain_ffn_term = rms_back(grad_normed_ffn, residual, scale_ffn, gain_ffn)
        grad_residual = grad_outer + grad_resid_part
        grad_branch = grad_residual.astype(jnp.bfloat16)
        grad_attended = (
            jnp.einsum("td,ed->te", grad_branch, full_out, preferred_element_type=jnp.float32)
            .astype(jnp.bfloat16)
            .reshape(tok_rows, H, HD)
        )
        grad_mixed = lax.all_to_all(grad_attended, "seq", split_axis=1, concat_axis=0, tiled=True)
        grad_proj_head, grad_logit_head, kernel_term, head_gain_term = mixer_back(
            grad_mixed.astype(jnp.float32)
        )
        grad_proj, grad_logits = (
            lax.all_to_all(
                grad_proj_head.astype(jnp.bfloat16), "seq", split_axis=0, concat_axis=2, tiled=True
            ),
            lax.all_to_all(
                grad_logit_head.astype(jnp.bfloat16), "seq", split_axis=0, concat_axis=2, tiled=True
            ),
        )
        grad_proj = grad_proj.reshape(tok_rows, 3 * D)
        grad_logits = grad_logits.reshape(tok_rows, H)
        grad_normed_in = jnp.einsum(
            "tc,dc->td", grad_proj, full_qkv, preferred_element_type=jnp.float32
        ) + jnp.einsum("th,dh->td", grad_logits, full_beta, preferred_element_type=jnp.float32)
        grad_in_part, gain_in_term = rms_back(grad_normed_in, rows_in, scale_in, gain_in)
        sent = (grad_residual + grad_in_part).astype(jnp.bfloat16)
        returned = pass_section(sent)
        if slot_index < micro:
            grad_rows[slot_index] = jnp.where(section_first, sent, returned)
        kernel_acc = kernel_acc + kernel_term
        gain_in_acc = gain_in_acc + gain_in_term
        gain_ffn_acc = gain_ffn_acc + gain_ffn_term
        head_gain_acc = head_gain_acc + head_gain_term
        kept[slot_index] = (
            normed_in,
            grad_proj,
            grad_logits,
            attended,
            grad_branch,
            ffn_rows,
            grad_gate,
            grad_up,
            hidden,
            grad_low,
        )

    def gather_kept(position):
        return jnp.concatenate(
            [
                jnp.where(section_first, kept[which][position], kept[which + 1][position])
                for which in range(micro)
            ],
            axis=0,
        )

    normed_all = gather_kept(0)
    grad_proj_all = gather_kept(1)
    grad_logit_all = gather_kept(2)
    attended_all = gather_kept(3)
    branch_all = gather_kept(4)
    ffn_rows_all = gather_kept(5)
    grad_gate_all = gather_kept(6)
    grad_up_all = gather_kept(7)
    hidden_all = gather_kept(8)
    ffn_grad_all = gather_kept(9)
    grad_qkv_full = jnp.einsum(
        "td,tc->dc", normed_all, grad_proj_all, preferred_element_type=jnp.float32
    )
    grad_beta_full = jnp.einsum(
        "td,th->dh", normed_all, grad_logit_all, preferred_element_type=jnp.float32
    )
    grad_out_full = jnp.einsum(
        "td,te->de", attended_all, branch_all, preferred_element_type=jnp.float32
    )
    grad_qkv_part, grad_beta_part, grad_out_part = (
        lax.psum_scatter(
            grad_qkv_full.astype(jnp.bfloat16), "fsdp", scatter_dimension=0, tiled=True
        ).astype(jnp.float32),
        lax.psum_scatter(
            grad_beta_full.astype(jnp.bfloat16), "fsdp", scatter_dimension=0, tiled=True
        ).astype(jnp.float32),
        lax.psum_scatter(
            grad_out_full.astype(jnp.bfloat16), "fsdp", scatter_dimension=0, tiled=True
        ).astype(jnp.float32),
    )
    ffn_part = lax.psum_scatter(
        jnp.stack(
            [
                jnp.einsum(
                    "tf,td->fd", grad_gate_all, ffn_rows_all, preferred_element_type=jnp.float32
                ),
                jnp.einsum(
                    "tf,td->fd", grad_up_all, ffn_rows_all, preferred_element_type=jnp.float32
                ),
                jnp.einsum(
                    "tf,td->fd", hidden_all, ffn_grad_all, preferred_element_type=jnp.float32
                ),
            ],
            axis=1,
        ).astype(jnp.bfloat16),
        "fsdp",
        scatter_dimension=0,
        tiled=True,
    ).astype(jnp.float32)
    grad_ffn_part = jnp.transpose(ffn_part[:, :2], (1, 2, 0))
    grad_down_part = ffn_part[:, 2]
    summed = (
        lax.psum(grad_qkv_part.astype(jnp.bfloat16), "seq").astype(jnp.float32),
        lax.psum(grad_beta_part.astype(jnp.bfloat16), "seq").astype(jnp.float32),
        lax.psum(grad_out_part.astype(jnp.bfloat16), "seq").astype(jnp.float32),
        lax.psum(grad_ffn_part.astype(jnp.bfloat16), "seq").astype(jnp.float32),
        lax.psum(grad_down_part.astype(jnp.bfloat16), "seq").astype(jnp.float32),
    )
    kernel_full = lax.dynamic_update_slice_in_dim(
        jnp.zeros((conv_w.shape[1], 3, D), jnp.float32), kernel_acc, head_start, 2
    )
    smaller = lax.psum((kernel_full, gain_in_acc, head_gain_acc, gain_ffn_acc), ("seq", "fsdp"))
    return (
        jnp.stack(block_rows)[:, None],
        jnp.stack(grad_rows)[:, None],
        smaller[1][None],
        summed[0][None],
        summed[1][None],
        smaller[0][None],
        smaller[2][None],
        summed[2][None],
        smaller[3][None],
        summed[3][None],
        summed[4][None],
    )


def solution(mesh):
    placed = (
        P(None, "fsdp", "seq", None),
        P(None, "fsdp", "seq", None),
        P(None, "fsdp", None),
        P(None, "fsdp", None),
        P("section", None),
        P("section", "fsdp", None),
        P("section", "fsdp", None),
        P("section", None, None, None),
        P("section", None),
        P("section", "fsdp", None),
        P("section", None),
        P("section", None, None, "fsdp"),
        P("section", "fsdp", None),
    )
    return jax.shard_map(
        local,
        mesh=mesh,
        in_specs=placed,
        out_specs=(
            P(None, "fsdp", "seq", None),
            P(None, "fsdp", "seq", None),
            P("section", None),
            P("section", "fsdp", None),
            P("section", "fsdp", None),
            P("section", None, None, None),
            P("section", None),
            P("section", "fsdp", None),
            P("section", None),
            P("section", None, None, "fsdp"),
            P("section", "fsdp", None),
        ),
        check_vma=False,
    )
```

profile of v0, /device:TPU:0, one launch (start us, length us, event | category | flops | bytes accessed | tf_op | source)
XLA Modules:
  0.0 1792.2 jit_solution(13547989817530182907)
XLA Ops:
  11.8 26.4 %all-gather = bf16[1,1024,8]{2,0,1:T(2,128)(2,1)S(1)} all-gather(bf16[1,64,8]{2,0,1:T(2,128)(2,1)S(1)} %copy.1167), channel_id=2, replica_groups=mesh['section'=2,'seq'=4,'fsdp'=16] {'fsdp'}, dimensions={1}, use_global_device_ids=true | all-gather | bytes 17408 | tf_op jit(solution)/shard_map/all_gather | solution.py:178
  57.4 17.2 all-gather.9.cloned.1.call-done
  85.2 6.8 all-to-all-done.1
  100.8 39.3 %custom-call.21 = f32[4,2,1,64,64]{3,4,2,1,0:T(8,128)S(1)} custom-call(f32[4,2,1,64,64]{4,3,2,1,0:T(8,128)S(1)} %add_bitcast_fusion.2), custom_call_target="InvertDiagBlocksLowerTriangular" | custom-call | tf_op jit(solution)/shard_map/jvp()/triangular_solve/custom-call.1 | solution.py:87
  142.2 13.6 while.150
  162.8 5.3 all-to-all-done.2
  171.1 67.5 %all-gather.7.cloned.1.call-done = bf16[3,1024,2816]{1,2,0:T(8,128)(2,1)} async-done(((bf16[3,1024,176]{1,2,0:T(8,128)(2,1)}), bf16[3,1024,2816]{1,2,0:T(8,128)(2,1)}) %all-gather.7.cloned.1.call-update) | async-done | bytes 17301520 | tf_op jit(solution)/shard_map/all_gather | solution.py:182
  243.3 5.6 multiply_convert_fusion.8
  272.0 6.4 all-to-all-done.4
  286.6 39.3 %custom-call.22 = f32[4,2,1,64,64]{3,4,2,1,0:T(8,128)S(1)} custom-call(f32[4,2,1,64,64]{4,3,2,1,0:T(8,128)S(1)} %add_bitcast_fusion.1), custom_call_target="InvertDiagBlocksLowerTriangular" | custom-call | tf_op jit(solution)/shard_map/jvp()/triangular_solve/custom-call.1 | solution.py:87
  334.2 38.9 %while.151 = (s32[]{:T(128)}, f32[2,128,128]{2,1,0:T(8,128)S(1)}, f32[4,2,64,128]{3,2,0,1:T(8,128)S(1)}, f32[4,2,128,128]{3,2,1,0:T(8,128)S(1)}, f32[4,1,64,1]{2...) while((s32[]{:T(128)}, f32[2,128,128]{2,1,0:T(8,128)S(1)}, ...), condition=%wide.region_17.19_spmd.clone, body=%wide.region_16.18_spmd.clone.sunk | while | flops 88375296 | bytes 1645805 | solution.py:121
  397.3 5.8 broadcast_select_fusion.3
  424.6 6.8 all-to-all-done.7
  436.8 5.2 fusion.550
  447.5 40.0 %custom-call.23 = f32[4,2,1,64,64]{3,4,2,1,0:T(8,128)S(1)} custom-call(f32[4,2,1,64,64]{4,3,2,1,0:T(8,128)} %add_bitcast_fusion), custom_call_target="InvertDiagBlocksLowerTriangular" | custom-call | tf_op jit(solution)/shard_map/jvp()/triangular_solve/custom-call.1 | solution.py:87
  502.8 37.7 %while.152 = (s32[]{:T(128)}, f32[2,128,128]{2,1,0:T(8,128)S(1)}, f32[4,2,64,128]{3,2,0,1:T(8,128)S(1)}, f32[4,2,128,128]{3,2,1,0:T(8,128)}, f32[4,1,64,1]{2,3,1...) while((s32[]{:T(128)}, f32[2,128,128]{2,1,0:T(8,128)S(1)}, ...), condition=%wide.region_27.29_spmd.clone, body=%wide.region_26.28_spmd.clone.sunk | while | flops 88375296 | bytes 1646061 | solution.py:121
  544.5 9.5 all_to_all.216
  562.7 5.5 broadcast_select_fusion.2
  596.4 25.7 %scatter_fusion = f32[256,2,128]{2,1,0:T(2,128)} fusion(f32[256,2,128]{2,1,0:T(2,128)} %broadcast.905.clone, s32[256]{0:T(256)} %bitcast.1362, f32[256,2,128]{2,1,0:T(2,128)} %copy.1244), kind=kCustom, calls=%fused_computation.12 | custom fusion | flops 65536 | bytes 787456 | tf_op jit(solution)/shard_map/transpose(jvp())/scatter-add | solution.py:148
  629.5 53.8 %while.153 = (s32[]{:T(128)}, f32[2,128,128]{2,1,0:T(8,128)S(1)}, f32[4,2,64,128]{3,2,1,0:T(8,128)}, f32[4,2,64,128]{3,2,1,0:T(8,128)}, f32[4,2,64,128]{3,2,1,0:...) while((s32[]{:T(128)}, f32[2,128,128]{2,1,0:T(8,128)S(1)}, ...), condition=%wide.region_34.36_spmd.clone, body=%wide.region_33.35_spmd.clone.sunk | while | flops 176488448 | bytes 2371319 | solution.py:121
  704.9 5.9 multiply_reduce_fusion.11
  728.3 20.0 %scatter_fusion.1 = f32[256,3,2,128]{3,2,1,0:T(2,128)S(1)} fusion(f32[256,3,2,128]{3,2,1,0:T(2,128)S(1)} %broadcast.903.clone, s32[256]{0:T(256)} %copy-done.177, f32[256,3,2,128]{3,2,1,0:T(2,128)} %fusion.337), kind=kCustom, calls=%fused_computation.13 | custom fusion | flops 196608 | bytes 2360320 | tf_op jit(solution)/shard_map/transpose(jvp())/scatter-add | solution.py:133
  749.3 4.9 all-to-all-start.10
  755.3 6.3 all-to-all-done.10
  764.2 5.0 fusion.226
  773.0 5.7 broadcast_select_fusion.4
  794.5 5.1 all-to-all-done.12
  800.7 16.4 scatter_fusion.2
  824.2 57.4 %while.154 = (s32[]{:T(128)}, f32[2,128,128]{2,1,0:T(8,128)S(1)}, f32[4,2,64,128]{3,2,1,0:T(8,128)}, f32[4,2,64,128]{3,2,1,0:T(8,128)}, f32[4,2,64,128]{3,2,1,0:...) while((s32[]{:T(128)}, f32[2,128,128]{2,1,0:T(8,128)S(1)}, ...), condition=%wide.region_46.50_spmd.clone, body=%wide.region_45.49_spmd.clone.sunk | while | flops 176488448 | bytes 2371827 | solution.py:121
  907.1 5.7 multiply_reduce_fusion.7
  926.0 20.0 %scatter_fusion.3 = f32[256,3,2,128]{3,2,1,0:T(2,128)S(1)} fusion(f32[256,3,2,128]{3,2,1,0:T(2,128)S(1)} %broadcast.903.clone.1, s32[256]{0:T(256)} %get-tuple-element.2736, f32[256,3,2,128]{3,2,1,0:T(2,128)} %fusion.339), kind=kCustom, calls=%fused_computation.16 | custom fusion | flops 196608 | bytes 2360320 | tf_op jit(solution)/shard_map/transpose(jvp())/scatter-add | solution.py:133
  953.4 5.9 all-to-all-done.13
  961.9 5.0 fusion.224
  970.9 5.6 broadcast_select_fusion.5
  990.9 5.3 convert_bitcast_fusion.1
  996.3 5.4 convert_bitcast_fusion.2
  1002.0 8.3 scatter_fusion.4
  1013.6 42.0 %while.155 = (s32[]{:T(128)}, f32[2,128,128]{2,1,0:T(8,128)S(1)}, f32[4,2,64,128]{3,2,1,0:T(8,128)}, f32[4,2,64,128]{3,2,1,0:T(8,128)}, f32[4,2,64,128]{3,2,1,0:...) while((s32[]{:T(128)}, f32[2,128,128]{2,1,0:T(8,128)S(1)}, ...), condition=%wide.region_58.62_spmd.clone, body=%wide.region_57.61_spmd.clone.sunk | while | flops 176488448 | bytes 2371575 | solution.py:121
  1067.6 5.3 convert_bitcast_fusion
  1075.0 14.2 pad_maximum_fusion
  1105.5 5.0 multiply_reduce_fusion.3
  1114.2 19.9 %scatter_fusion.5 = f32[256,3,2,128]{3,2,1,0:T(2,128)S(1)} fusion(f32[256,3,2,128]{3,2,1,0:T(2,128)S(1)} %broadcast.903, s32[256]{0:T(256)S(1)} %copy-done.179, f32[256,3,2,128]{3,2,1,0:T(2,128)} %fusion.341), kind=kCustom, calls=%fused_computation.19 | custom fusion | flops 196608 | bytes 2360320 | tf_op jit(solution)/shard_map/transpose(jvp())/scatter-add | solution.py:133
  1134.4 11.8 all_to_all.217
  1159.7 9.1 psum.65
  1169.4 93.6 %reduce-scatter.11.cloned.1.call-done = bf16[176,3,1024]{2,0,1:T(8,128)(2,1)} async-done(((bf16[2816,3,1024]{2,0,1:T(8,128)(2,1)}), bf16[176,3,1024]{2,0,1:T(8,128)(2,1)}) %reduce-scatter.11.cloned.1.call-update) | async-done | bytes 1081360 | tf_op jit(solution)/shard_map/reduce_scatter | solution.py:372
  1266.8 73.3 %reduce-scatter.9.cloned.1.call-done = bf16[64,1024]{1,0:T(8,128)(2,1)} async-done(((bf16[1024,1024]{1,0:T(8,128)(2,1)}), bf16[64,1024]{1,0:T(8,128)(2,1)}) %reduce-scatter.9.cloned.1.call-update) | async-done | bytes 131088 | tf_op jit(solution)/shard_map/reduce_scatter | solution.py:368
  1340.1 84.4 %reduce-scatter.7.cloned.1.call-done = bf16[64,3072]{1,0:T(8,128)(2,1)} async-done(((bf16[1024,3072]{1,0:T(8,128)(2,1)}), bf16[64,3072]{1,0:T(8,128)(2,1)}) %reduce-scatter.7.cloned.1.call-update) | async-done | bytes 393232 | tf_op jit(solution)/shard_map/reduce_scatter | solution.py:362
  1430.0 346.6 %all-reduce.54 = (f32[1,1024]{1,0:T(1,128)}, f32[1,4,3,1024]{3,1,2,0:T(4,128)}, f32[1,128]{1,0:T(1,128)}, f32[1,1024]{1,0:T(1,128)}) all-reduce(f32[1,1024]{1,0:T(1,128)S(1)} %bitcast.1342, f32[1,4,3,1024]{3,1,2,0:T(4,128)S(1)} %constant_dynamic-update-slice_fusion.6, ...), channel_id=1, replica_groups=mesh['section'=2,'seq'=4,'fsdp'=16] {'seq','fsdp'}, use_global_device_ids=true, to_apply=%region_69.73 | all-reduce | flops 14464 | bytes 115712 | tf_op jit(solution)/shard_map/psum | solution.py:403
  (1163 shorter events, 667.0 us)
Async XLA Ops:
  7.2 67.4 %all-gather.9.cloned.1.call-start = ((), (), s32[]{:S(2)}) async-start(), calls=%async_computation.26 | async-start | bytes 6684672 | tf_op jit(solution)/shard_map/all_gather | solution.py:177
  7.9 160.4 %all-gather.11.cloned.1.call-start = ((), (), s32[]{:S(2)}) async-start(), calls=%async_computation.27 | async-start | bytes 2228224 | tf_op jit(solution)/shard_map/all_gather | solution.py:179
  8.7 230.0 %all-gather.7.cloned.1.call-start = ((), (), s32[]{:S(2)}) async-start(), calls=%async_computation.22 | async-start | bytes 18382848 | tf_op jit(solution)/shard_map/all_gather | solution.py:182
  38.5 216.7 %copy-start.104 = (bf16[1,1024,8]{1,2,0:T(8,128)(2,1)}, bf16[1,1024,8]{1,2,0:T(8,128)(2,1)S(1)}, u32[]{:S(2)}) copy-start(bf16[1,1024,8]{1,2,0:T(8,128)(2,1)S(1)} %copy.1168) | copy-start | bytes 49156
  41.8 37.7 %all-to-all-start = ((bf16[64,1,8]{0,1,2:T(2,128)(2,1)}), bf16[64,1,8]{0,1,2:T(2,128)(2,1)S(1)}, u32[]{:S(2)}, u32[]{:S(2)}) async-start(bf16[64,1,8]{0,1,2:T(2,128)(2,1)} %copy.1169), calls=%async_computation | async-start | bytes 8192 | tf_op jit(solution)/shard_map/all_to_all | solution.py:210
  55.5 225.4 %copy-start.109 = (f32[1,1,3,256]{3,1,2,0:T(1,128)}, f32[1,1,3,256]{3,1,2,0:T(1,128)S(1)}, u32[]{:S(2)}) copy-start(f32[1,1,3,256]{3,1,2,0:T(1,128)S(1)} %get-tuple-element.2656) | copy-start | bytes 9220
  55.5 225.4 %copy-start.112 = (f32[1,1,3,256]{3,1,2,0:T(1,128)}, f32[1,1,3,256]{3,1,2,0:T(1,128)S(1)}, u32[]{:S(2)}) copy-start(f32[1,1,3,256]{3,1,2,0:T(1,128)S(1)} %get-tuple-element.2657) | copy-start | bytes 9220
  55.5 225.4 %copy-start.115 = (f32[1,1,3,256]{3,1,2,0:T(1,128)}, f32[1,1,3,256]{3,1,2,0:T(1,128)S(1)}, u32[]{:S(2)}) copy-start(f32[1,1,3,256]{3,1,2,0:T(1,128)S(1)} %get-tuple-element.2658) | copy-start | bytes 9220
  55.5 230.9 %copy-start.96 = (f32[64,64]{1,0:T(8,128)}, f32[64,64]{1,0:T(8,128)S(1)}, u32[]{:S(2)}) copy-start(f32[64,64]{1,0:T(8,128)S(1)} %fusion.508) | copy-start | bytes 49156
  56.4 230.0 %copy-start.98 = (f32[64,64]{1,0:T(8,128)}, f32[64,64]{1,0:T(8,128)S(1)}, u32[]{:S(2)}) copy-start(f32[64,64]{1,0:T(8,128)S(1)} %get-tuple-element.2743) | copy-start | bytes 49156
  57.4 229.0 %copy-start.80 = (f32[4,64,64]{2,1,0:T(8,128)}, f32[4,64,64]{2,1,0:T(8,128)S(1)}, u32[]{:S(2)}) copy-start(f32[4,64,64]{2,1,0:T(8,128)S(1)} %get-tuple-element.2663) | copy-start | bytes 196612
  57.4 271.3 %copy-start.63 = (f32[4,64,64]{2,1,0:T(8,128)}, f32[4,64,64]{2,1,0:T(8,128)S(1)}, u32[]{:S(2)}) copy-start(f32[4,64,64]{2,1,0:T(8,128)S(1)} %get-tuple-element.2666) | copy-start | bytes 196612
  79.5 12.5 all-to-all-start.1
  142.2 96.5 %copy-start.126 = (f32[1,1024]{1,0:T(1,128)S(1)}, f32[1,1024]{1,0:T(1,128)}, u32[]{:S(2)}) copy-start(f32[1,1024]{1,0:T(1,128)} %param.41) | copy-start | bytes 12292
  158.5 9.5 all-to-all-start.2
  252.9 1.5 collective-permute-start
  256.0 9.5 all-to-all-start.3
  265.5 12.9 all-to-all-start.4
  377.2 9.3 all-to-all-start.5
  407.1 1.4 collective-permute-start.1
  410.1 8.8 all-to-all-start.6
  418.9 12.5 all-to-all-start.7
  583.6 10.2 all-to-all-start.9
  720.5 28.8 %all-to-all-start.11 = ((bf16[256,1,2]{2,1,0:T(2,128)(2,1)}), bf16[256,1,2]{2,1,0:T(2,128)(2,1)}, u32[]{:S(2)}, u32[]{:S(2)}) async-start(bf16[256,1,2]{2,1,0:T(2,128)(2,1)} %copy.1276), calls=%async_computation.11 | async-start | bytes 262144 | tf_op jit(solution)/shard_map/all_to_all | solution.py:302
  749.3 12.3 all-to-all-start.10
  770.9 1.4 collective-permute-start.3
  790.2 9.4 all-to-all-start.12
  919.1 28.0 %all-to-all-start.14 = ((bf16[256,1,2]{2,1,0:T(2,128)(2,1)}), bf16[256,1,2]{2,1,0:T(2,128)(2,1)S(1)}, u32[]{:S(2)}, u32[]{:S(2)}) async-start(bf16[256,1,2]{2,1,0:T(2,128)(2,1)} %copy.1314), calls=%async_computation.14 | async-start | bytes 262144 | tf_op jit(solution)/shard_map/all_to_all | solution.py:302
  947.0 12.3 all-to-all-start.13
  969.1 1.7 collective-permute-start.4
  987.2 14.5 all-to-all-start.15
  1062.9 10.7 all-to-all-start.17
  1067.6 91.3 %reduce-scatter.13.cloned.1.call-start = ((), (), s32[]{:S(2)}) async-start(), calls=%async_computation.28 | async-start | bytes 278528
  1074.9 188.1 %reduce-scatter.11.cloned.1.call-start = ((), (), s32[]{:S(2)}) async-start(), calls=%async_computation.25 | async-start | bytes 18382848 | tf_op jit(solution)/shard_map/reduce_scatter | solution.py:372
  1089.3 250.8 %reduce-scatter.9.cloned.1.call-start = ((), (), s32[]{:S(2)}) async-start(), calls=%async_computation.24 | async-start | bytes 2228224 | tf_op jit(solution)/shard_map/reduce_scatter | solution.py:368
  1092.4 332.1 %reduce-scatter.7.cloned.1.call-start = ((), (), s32[]{:S(2)}) async-start(), calls=%async_computation.23 | async-start | bytes 6684672 | tf_op jit(solution)/shard_map/reduce_scatter | solution.py:362
  1151.7 625.6 %all-reduce.58.cloned.1.call-start = ((), (), s32[]{:S(2)}) async-start(), calls=%async_computation.29 | async-start | bytes 3211264 | tf_op jit(solution)/shard_map/psum | solution.py:394
  1156.4 1.4 collective-permute-start.2
  1157.8 271.5 %copy-start.37 = (bf16[2,1,64,1024]{3,2,1,0:T(8,128)(2,1)S(1)}, bf16[2,1,64,1024]{3,2,1,0:T(8,128)(2,1)}, u32[]{:S(2)}) copy-start(bf16[2,1,64,1024]{3,2,1,0:T(8,128)(2,1)} %param.31) | copy-start | bytes 786436
  1157.9 271.5 %copy-start.108 = (bf16[1,1024,8]{1,2,0:T(8,128)(2,1)S(1)}, bf16[1,1024,8]{1,2,0:T(8,128)(2,1)}, u32[]{:S(2)}) copy-start(bf16[1,1024,8]{1,2,0:T(8,128)(2,1)} %copy-done.104) | copy-start | bytes 49156
  1157.9 271.5 %copy-start.151 = (bf16[64,1,4,2]{0,3,2,1:T(2,128)(2,1)S(1)}, bf16[64,1,4,2]{0,3,2,1:T(2,128)(2,1)}, u32[]{:S(2)}) copy-start(bf16[64,1,4,2]{0,3,2,1:T(2,128)(2,1)} %copy-done.150) | copy-start | bytes 3076
  1157.9 271.5 %copy-start.184 = (f32[64]{0:T(128)S(1)}, f32[64]{0:T(128)}, u32[]{:S(2)}) copy-start(f32[64]{0:T(128)} %copy-done.183) | copy-start | bytes 772
  1158.8 271.0 %copy-start.49 = (f32[64,1024]{1,0:T(8,128)S(1)}, f32[64,1024]{1,0:T(8,128)}, u32[]{:S(2)}) copy-start(f32[64,1024]{1,0:T(8,128)} %copy-done.48) | copy-start | bytes 786436
  1158.8 271.0 %copy-start.201 = (f32[64]{0:T(128)S(1)}, f32[64]{0:T(128)}, u32[]{:S(2)}) copy-start(f32[64]{0:T(128)} %get-tuple-element.2696) | copy-start | bytes 772
  1264.7 165.2 %copy-start.165 = (f32[1024]{0:T(1024)S(1)}, f32[1024]{0:T(1024)}, u32[]{:S(2)}) copy-start(f32[1024]{0:T(1024)} %get-tuple-element.2325) | copy-start | bytes 12292
  1264.7 165.2 %copy-start.166 = (f32[1024]{0:T(1024)S(1)}, f32[1024]{0:T(1024)}, u32[]{:S(2)}) copy-start(f32[1024]{0:T(1024)} %get-tuple-element.2323) | copy-start | bytes 12292
  1264.7 511.9 %copy-start.100 = (bf16[1,64,1024]{2,1,0:T(8,128)(2,1)S(1)}, bf16[1,64,1024]{2,1,0:T(8,128)(2,1)}, u32[]{:S(2)}) copy-start(bf16[1,64,1024]{2,1,0:T(8,128)(2,1)} %get-tuple-element.2650) | copy-start | bytes 393220
  1429.9 346.7 %collective-permute-start.5 = (bf16[64,1024]{1,0:T(8,128)(2,1)S(1)}, bf16[64,1024]{1,0:T(8,128)(2,1)S(1)}, u32[]{:S(2)}, u32[]{:S(2)}) collective-permute-start(bf16[64,1024]{1,0:T(8,128)(2,1)S(1)} %fusion.401), channel_id=1, source_target_pairs={{0,64},{64,0},{1,65},{65,1},{2,66},{66,2},{3,67},{67,3},{4,68},{68... | collective-permute-start | bytes 393224 | tf_op jit(solution)/shard_map/ppermute | solution.py:21
  (205 other events, 4156.9 us)
Sparse Core Ops, SparseCore 0:
  10.2 64.3 all-gather.8
  76.7 45.9 all-gather.10
  125.4 113.1 all-gather.6
  1075.0 71.5 reduce-scatter.12
  1150.3 112.6 reduce-scatter.10
  1266.1 73.9 reduce-scatter.8
  1343.9 80.5 reduce-scatter.6
  1428.4 50.4 all-reduce.57
where the time goes:
time: 1810 us; the launch traced here: 1790 us
  blocking collectives  403 us (22%)
  waiting for transfers between devices  391 us (22%)
  other arithmetic  373 us (21%)
  matrix products  362 us (20%)
  local copies, waits for them, and re-layouts  177 us (10%)
  starting transfers between devices  67.8 us (4%)
  between operations  18.2 us (1%)
    psum x1, blocking collectives, local(): lax.psum((kernel_full, gain_in_acc, head_gain_acc, gain_ffn_acc), ('seq',...  347 us
    dot_general x162, matrix products, exact_einsum(): jnp.einsum(form, left_side, right_side, precision=lax.Precision.HIGHEST)  197 us
    another operation x9, other arithmetic, delta_blocks(): lax.linalg.triangular_solve(system, sources, left_side=True, lower=True,...  120 us
    reduce_scatter x1, waiting for transfers between devices, local(): lax.psum_scatter(jnp.stack([jnp.einsum('tf,td->fd', grad_gate_all, ffn_ro...  93.6 us
    reduce_scatter x1, waiting for transfers between devices, local(): lax.psum_scatter(grad_qkv_full.astype(jnp.bfloat16), 'fsdp', scatter_dime...  84.4 us
    reduce_scatter x1, waiting for transfers between devices, local(): lax.psum_scatter(grad_out_full.astype(jnp.bfloat16), 'fsdp', scatter_dime...  73.3 us
    all_gather x1, waiting for transfers between devices, local(): full_ffn = lax.all_gather(stacked, 'fsdp', axis=2, tiled=True)  67.5 us
    scatter-add x3, other arithmetic, mixer_local(): series = projected[inverse]  59.9 us
  transfers between devices with their start and end apart: 30, of which 20 were waited for; matrix products, arithmetic and copies ran while one was open for 14% of the time, Pallas kernels for 0%

commit v1 on v0

v1 whole, which is shorter than its diff:
```python
import functools

import jax
import jax.numpy as jnp
from jax import lax
from jax.experimental import pallas as pl
from jax.experimental.pallas import tpu as pltpu
from jax.sharding import PartitionSpec as P

D = 1024
H = 8
HD = 128
PACK = 256
ROWS = 64
UNIT = 48
QW = 896
MESH = pl.DeviceIdType.MESH
F32, BF16 = jnp.float32, jnp.bfloat16
VMEM = pl.BlockSpec(memory_space=pltpu.VMEM)
SMEM = pl.BlockSpec(memory_space=pltpu.SMEM)
ANY = pl.BlockSpec(memory_space=pl.ANY)
VMEM_BYTES = 60 * 1024 * 1024


def sds(shape, dtype):
    return jax.ShapeDtypeStruct(shape, dtype)


def dot(left, right, dims):
    return lax.dot_general(left, right, (dims, ((), ())), preferred_element_type=F32)


NN = ((1,), (0,))
NT = ((1,), (1,))
TN = ((0,), (0,))


def halves(value):
    high = value.astype(BF16)
    return high, (value - high.astype(F32)).astype(BF16)


def dot3(left, right, dims):
    return dot(left[0], right[0], dims) + (
        dot(left[0], right[1], dims) + dot(left[1], right[0], dims)
    )


def place():
    fsdp = lax.axis_index("fsdp")
    return (
        lax.axis_index("section"),
        lax.axis_index("seq"),
        lax.div(fsdp, 4),
        lax.rem(fsdp, 4),
    )


def along_x(seq, step):
    return {"seq": lax.rem(seq + step, 4)}


def along_y(z, y, step):
    return {"fsdp": z * 4 + lax.rem(y + step, 4)}


def along_z(z, y, step):
    return {"fsdp": lax.rem(z + step, 4) * 4 + y}


def greet(peers):
    barrier = pltpu.get_barrier_semaphore()
    for peer in peers:
        pl.semaphore_signal(barrier, inc=1, device_id=peer, device_id_type=MESH)
    pl.semaphore_wait(barrier, len(peers))


def remote(source, target, send, recv, peer):
    return pltpu.make_async_remote_copy(
        src_ref=source,
        dst_ref=target,
        send_sem=send,
        recv_sem=recv,
        device_id=peer,
        device_id_type=MESH,
    )


class RingGather:
    def __init__(self, me, right, left, own, slot, send, recv):
        self.at_left, self.at_right = lax.rem(me + 3, 4), lax.rem(me + 1, 4)
        self.opposite = lax.rem(me + 2, 4)
        self.slot = slot

        def copy(index, half, source, peer, sem):
            return remote(source, slot(index, half), send.at[sem], recv.at[sem], peer)

        self.first = [
            copy(me, 0, own(0), right, 0),
            copy(me, 1, own(1), left, 1),
            copy(me, 1, own(1), right, 2),
            copy(me, 0, own(0), left, 3),
        ]
        self.second = [
            copy(self.at_left, 0, slot(self.at_left, 0), right, 4),
            copy(self.at_right, 1, slot(self.at_right, 1), left, 5),
        ]

    def start(self):
        for copy in self.first:
            copy.start()

    def middle(self):
        self.first[0].wait_recv()
        self.second[0].start()
        self.first[1].wait_recv()
        self.second[1].start()

    def near(self):
        self.first[2].wait_recv()
        self.first[3].wait_recv()

    def far(self):
        self.second[0].wait_recv()
        self.second[1].wait_recv()

    def finish(self):
        for copy in self.first + self.second:
            copy.wait_send()


class RingReduce:
    def __init__(self, me, right, left, part, near, from_left, from_right, send, recv):
        at_right, at_left = lax.rem(me + 1, 4), lax.rem(me + 3, 4)
        opposite = lax.rem(me + 2, 4)
        self.me, self.part, self.near = me, part, near
        self.from_left, self.from_right = from_left, from_right
        self.at_right, self.at_left = at_right, at_left

        def copy(source, target, peer, sem):
            return remote(source, target, send.at[sem], recv.at[sem], peer)

        self.first = [
            copy(part(opposite, 0), near(0), right, 0),
            copy(part(opposite, 1), near(1), left, 1),
            copy(part(at_right, 1), from_left(1), right, 2),
            copy(part(at_left, 0), from_right(0), left, 3),
        ]
        self.second = [
            copy(part(at_right, 0), from_left(0), right, 4),
            copy(part(at_left, 1), from_right(1), left, 5),
        ]

    def start(self):
        for copy in self.first:
            copy.start()

    def middle(self):
        for half, index in ((0, self.at_right), (1, self.at_left)):
            self.first[half].wait_recv()
            add_into(self.part(index, half), [self.near(half)])
            self.second[half].start()

    def arrive(self):
        for copy in (self.first[2], self.first[3], self.second[0], self.second[1]):
            copy.wait_recv()

    def finish(self):
        for copy in self.first + self.second:
            copy.wait_send()

    def total(self):
        for half in (0, 1):
            add_into(self.part(self.me, half), [self.from_left(half), self.from_right(half)])


def add_into(target, others):
    shape = target.shape
    if len(shape) == 2:
        rows = 16
        steps = shape[0] // rows

        def body(step, carry):
            at = pl.ds(pl.multiple_of(step * rows, rows), rows)
            value = target[at, :].astype(F32)
            for other in others:
                value = value + other[at, :].astype(F32)
            target[at, :] = value.astype(target.dtype)
            return carry

        lax.fori_loop(0, steps, body, 0)
    else:
        for index in range(shape[0]):
            add_into(target.at[index], [other.at[index] for other in others])


def spread_kernel(
    x_ref,
    cot_ref,
    small_ref,
    q_ref,
    f_ref,
    o_ref,
    x_out,
    cot_out,
    small_out,
    q_out,
    f_out,
    o_out,
    send,
    recv,
    local,
    o_send,
    o_recv,
    pair_send,
    pair_recv,
):
    core, seq, z, y = place()
    partner = {"section": 1 - core}
    greet(
        [along_x(seq, k) for k in (1, 3)]
        + [along_y(z, y, k) for k in (1, 3)]
        + [along_z(z, y, k) for k in (1, 2, 3)]
        + [partner]
    )

    def cut(half, low):
        return pl.ds(low * half, low)

    own_copies = [
        pltpu.make_async_copy(x_ref, x_out.at[seq], local.at[0]),
        pltpu.make_async_copy(cot_ref, cot_out.at[seq], local.at[1]),
        pltpu.make_async_copy(small_ref, small_out.at[core], local.at[2]),
        pltpu.make_async_copy(q_ref, q_out.at[core, z, y], local.at[3]),
        pltpu.make_async_copy(f_ref, f_out.at[core, :, z, y], local.at[4]),
    ]
    for copy in own_copies:
        copy.start()

    def x_ring(source, target, sem):
        return RingGather(
            seq,
            along_x(seq, 1),
            along_x(seq, 3),
            lambda half: source.at[cut(half, 32)],
            lambda index, half: target.at[index, cut(half, 32)],
            send.at[sem],
            recv.at[sem],
        )

    def y_ring(own, slot, sem):
        return RingGather(
            y, along_y(z, y, 1), along_y(z, y, 3), own, slot, send.at[sem], recv.at[sem]
        )

    def z_ring(own, slot, sem):
        return RingGather(
            z, along_z(z, y, 1), along_z(z, y, 3), own, slot, send.at[sem], recv.at[sem]
        )

    rows_ring = x_ring(x_ref, x_out, 0)
    cot_ring = x_ring(cot_ref, cot_out, 1)
    pair_small = remote(
        small_ref, small_out.at[core], pair_send.at[0], pair_recv.at[0], partner
    )
    o_copies = [
        remote(o_ref, o_out.at[core, y], o_send.at[k], o_recv.at[0], along_z(z, y, k + 1))
        for k in range(3)
    ]
    own_o = pltpu.make_async_copy(o_ref, o_out.at[core, y], local.at[5])

    q_one = z_ring(
        lambda half: q_ref.at[cut(half, 32)],
        lambda index, half: q_out.at[core, index, y, cut(half, 32)],
        2,
    )
    d_one = z_ring(
        lambda half: f_ref.at[2, pl.ds(32 * half, 32 - 16 * half)],
        lambda index, half: f_out.at[core, 2, index, y, pl.ds(32 * half, 32 - 16 * half)],
        3,
    )
    g_one = y_ring(
        lambda half: f_ref.at[half], lambda index, half: f_out.at[core, half, z, index], 4
    )
    q_two = y_ring(
        lambda half: q_out.at[core, cut(half, 2), y],
        lambda index, half: q_out.at[core, cut(half, 2), index],
        5,
    )
    d_two = y_ring(
        lambda half: f_out.at[core, 2, cut(half, 2), y],
        lambda index, half: f_out.at[core, 2, cut(half, 2), index],
        6,
    )
    g_two = z_ring(
        lambda half: f_out.at[core, half, z], lambda index, half: f_out.at[core, half, index], 7
    )
    o_two = y_ring(
        lambda half: o_out.at[core, y, cut(half, 32)],
        lambda index, half: o_out.at[core, index, cut(half, 32)],
        8,
    )

    pair_small.start()
    rows_ring.start()
    q_one.start()
    g_one.start()

    @pl.when(z == seq)
    def _():
        own_o.start()
        for copy in o_copies:
            copy.start()

    d_one.start()
    cot_ring.start()

    rows_ring.middle()
    q_one.middle()
    g_one.middle()
    d_one.middle()
    cot_ring.middle()

    for copy in own_copies:
        copy.wait()

    sent = []

    def to_partner(piece):
        index = len(sent) + 1
        copy = remote(piece, piece, pair_send.at[index], pair_recv.at[index], partner)
        copy.start()
        sent.append(copy)

    q_one.near()
    q_one.far()
    q_two.start()
    to_partner(q_out.at[core, :, y])
    g_one.near()
    g_one.far()
    g_two.start()
    to_partner(f_out.at[core, 0, z])
    to_partner(f_out.at[core, 1, z])

    @pl.when(z == seq)
    def _():
        own_o.wait()
        for copy in o_copies:
            copy.wait_send()

    @pl.when(z != seq)
    def _():
        o_copies[0].wait_recv()

    o_two.start()
    to_partner(o_out.at[core, y])
    d_one.near()
    d_one.far()
    d_two.start()
    to_partner(f_out.at[core, 2, :, y])

    two = [
        (q_two, lambda index, half: q_out.at[core, cut(half, 2), index]),
        (g_two, lambda index, half: f_out.at[core, half, index]),
        (o_two, lambda index, half: o_out.at[core, index, cut(half, 32)]),
        (d_two, lambda index, half: f_out.at[core, 2, cut(half, 2), index]),
    ]
    for ring, piece in two:
        ring.middle()
        to_partner(piece(ring.at_left, 0))
        to_partner(piece(ring.at_right, 1))
    for ring, piece in two:
        ring.near()
        to_partner(piece(ring.at_left, 1))
        to_partner(piece(ring.at_right, 0))
        ring.far()
        to_partner(piece(ring.opposite, 0))
        to_partner(piece(ring.opposite, 1))
    for ring in (rows_ring, cot_ring):
        ring.near()
        ring.far()
    for ring in (rows_ring, cot_ring, q_one, d_one, g_one, q_two, d_two, g_two, o_two):
        ring.finish()
    pair_small.wait()
    for copy in sent:
        copy.wait()


def spread(x, cot, small, q, f, o):
    return pl.pallas_call(
        spread_kernel,
        out_shape=[
            sds((4, ROWS, D), BF16),
            sds((4, ROWS, D), BF16),
            sds((2, 16, D), F32),
            sds((2, 4, 4, 64, QW), BF16),
            sds((2, 3, 4, 4, UNIT, D), BF16),
            sds((2, 4, 64, D), BF16),
        ],
        in_specs=[ANY] * 6,
        out_specs=[ANY] * 6,
        scratch_shapes=[
            pltpu.SemaphoreType.DMA((9, 6)),
            pltpu.SemaphoreType.DMA((9, 6)),
            pltpu.SemaphoreType.DMA((6,)),
            pltpu.SemaphoreType.DMA((3,)),
            pltpu.SemaphoreType.DMA((1,)),
            pltpu.SemaphoreType.DMA((30,)),
            pltpu.SemaphoreType.DMA((30,)),
        ],
        compiler_params=pltpu.CompilerParams(collective_id=1, has_side_effects=True),
        name="spread",
    )(x, cot, small, q, f, o)


def rms(value):
    return lax.rsqrt(jnp.mean(value * value, axis=-1, keepdims=True) + 1e-06)


def rms_back(grad, value, scale, gain):
    weighted = grad * gain
    inner = jnp.mean(weighted * value, axis=-1, keepdims=True)
    return (
        scale * weighted - value * (scale * scale * scale) * inner,
        jnp.sum(grad * value * scale, axis=0, keepdims=True),
    )


def seq_reduce(part, own, near, from_left, from_right, send, recv, seq):
    own[...] = part[...]
    ring = RingReduce(
        seq,
        along_x(seq, 1),
        along_x(seq, 3),
        lambda index, half: own.at[index, pl.ds(32 * half, 32)],
        lambda half: near.at[half],
        lambda half: from_left.at[pl.ds(32 * half, 32)],
        lambda half: from_right.at[pl.ds(32 * half, 32)],
        send,
        recv,
    )
    ring.start()
    ring.middle()
    ring.arrive()
    total = (
        own[seq].astype(F32) + from_left[...].astype(F32) + from_right[...].astype(F32)
    )
    return ring, total


def seq_gather(out, send, recv, seq):
    ring = RingGather(
        seq,
        along_x(seq, 1),
        along_x(seq, 3),
        lambda half: out.at[seq, pl.ds(32 * half, 32)],
        lambda index, half: out.at[index, pl.ds(32 * half, 32)],
        send,
        recv,
    )
    ring.start()
    ring.middle()
    ring.near()
    ring.far()
    ring.finish()


def attended_kernel(part, rows, small, residual_out, gathered, *scratch, layer):
    *bufs, send, recv = scratch
    seq = lax.axis_index("seq")
    greet([along_x(seq, 1), along_x(seq, 3)])
    ring, total = seq_reduce(part, *bufs, send.at[0], recv.at[0], seq)
    residual = rows[seq].astype(F32) + total
    residual_out[...] = residual
    gathered[seq] = (residual * rms(residual) * small[layer, 1:2, :]).astype(BF16)
    seq_gather(gathered, send.at[1], recv.at[1], seq)
    ring.finish()


def output_kernel(part, residual, gathered, *scratch):
    *bufs, send, recv = scratch
    seq = lax.axis_index("seq")
    greet([along_x(seq, 1), along_x(seq, 3)])
    ring, total = seq_reduce(part, *bufs, send.at[0], recv.at[0], seq)
    gathered[seq] = (residual[...] + total).astype(BF16)
    seq_gather(gathered, send.at[1], recv.at[1], seq)
    ring.finish()


def last_output_kernel(part, residual, out, *scratch):
    *bufs, send, recv = scratch
    seq = lax.axis_index("seq")
    greet([along_x(seq, 1), along_x(seq, 3)])
    ring, total = seq_reduce(part, *bufs, send.at[0], recv.at[0], seq)
    out[...] = (residual[...] + total).astype(BF16)
    ring.finish()


def back_ffn_kernel(part, outer, residual, small, grad_out, gathered, gain_out, *scratch, layer):
    *bufs, send, recv = scratch
    seq = lax.axis_index("seq")
    greet([along_x(seq, 1), along_x(seq, 3)])
    ring, total = seq_reduce(part, *bufs, send.at[0], recv.at[0], seq)
    value = residual[...]
    grad, gain = rms_back(total, value, rms(value), small[layer, 1:2, :])
    grad = outer[seq].astype(F32) + grad
    grad_out[...] = grad
    gathered[seq] = grad.astype(BF16)
    gain_out[...] = gain
    seq_gather(gathered, send.at[1], recv.at[1], seq)
    ring.finish()


def back_in_kernel(part, grad_ref, rows, small, gathered, gain_out, *scratch, layer, last):
    *bufs, send, recv = scratch
    seq = lax.axis_index("seq")
    greet([along_x(seq, 1), along_x(seq, 3)])
    ring, total = seq_reduce(part, *bufs, send.at[0], recv.at[0], seq)
    value = rows[seq].astype(F32)
    grad, gain = rms_back(total, value, rms(value), small[layer, 0:1, :])
    grad = (grad_ref[...] + grad).astype(BF16)
    gain_out[...] = gain
    if last:
        gathered[...] = grad
    else:
        gathered[seq] = grad
        seq_gather(gathered, send.at[1], recv.at[1], seq)
    ring.finish()


def seq_call(kernel, out_shape, collective_id, name, *operands):
    return pl.pallas_call(
        kernel,
        out_shape=out_shape,
        in_specs=[VMEM] * len(operands),
        out_specs=[VMEM] * len(out_shape),
        scratch_shapes=[
            pltpu.VMEM((4, ROWS, D), BF16),
            pltpu.VMEM((2, 32, D), BF16),
            pltpu.VMEM((ROWS, D), BF16),
            pltpu.VMEM((ROWS, D), BF16),
            pltpu.SemaphoreType.DMA((2, 6)),
            pltpu.SemaphoreType.DMA((2, 6)),
        ],
        compiler_params=pltpu.CompilerParams(
            collective_id=collective_id, has_side_effects=True, vmem_limit_bytes=VMEM_BYTES
        ),
        name=name,
    )(*operands)


def shifted(value, step):
    rows = value.shape[0]
    filler = jnp.zeros((abs(step), value.shape[1]), value.dtype)
    if step > 0:
        return jnp.concatenate([filler, value[: rows - step]], axis=0)
    return jnp.concatenate([value[-step:], filler], axis=0)


def doc_places(doc_len):
    col = lax.broadcasted_iota(jnp.int32, (PACK, 1), 0)
    row = lax.broadcasted_iota(jnp.int32, (1, PACK), 1)
    start_col, start_row = jnp.zeros_like(col), jnp.zeros_like(row)
    end = 0
    for doc in range(4):
        end = end + doc_len[doc]
        start_col = jnp.where(col >= end, end, start_col)
        start_row = jnp.where(row >= end, end, start_row)
    return col - start_col, start_col == start_row


def one_hot(column, row):
    return (column == row).astype(F32).astype(BF16)


def sigmoid(value):
    return 1.0 / (1.0 + jnp.exp(-value))


def conv_taps(small_ref, layer, tap, part):
    return small_ref[layer, 4 + tap * 3 + part : 5 + tap * 3 + part, 0:256]


def conv_part(series, small_ref, layer, part, offset):
    total = series * conv_taps(small_ref, layer, 0, part)
    for tap in range(1, 4):
        moved = jnp.where(offset >= tap, shifted(series, tap), 0.0)
        total = total + moved * conv_taps(small_ref, layer, tap, part)
    return total


def inverse(system):
    col = lax.broadcasted_iota(jnp.int32, (PACK, PACK), 0)
    row = lax.broadcasted_iota(jnp.int32, (PACK, PACK), 1)
    apart = col ^ row
    result = jnp.where(col == row, 1.0, 0.0) - jnp.where(apart == 1, system, 0.0)
    high, low = halves(system)
    for level in range(1, 8):
        mask = (apart >> level) == 1
        corner = halves(jnp.where(mask, system, 0.0))
        now = halves(result)
        inner = halves(dot3(corner, now, NN))
        result = result - dot3(now, inner, NN)
    return result


def unit(value):
    scale = lax.rsqrt(jnp.sum(value * value, axis=-1, keepdims=True) + 1e-06)
    return value * scale, scale


def mixer_kernel(
    rows, w_q, w_o, small, perm_row, perm_col, doc_len, part, proj_out, inv_out, u_out, o_out, att_out, n_out, *, layer
):
    x = rows[...].astype(F32)
    normed = (x * rms(x) * small[layer, 0:1, :]).astype(BF16)
    n_out[...] = normed
    proj = dot(normed, w_q[...], NN).astype(BF16)
    place_col = lax.broadcasted_iota(jnp.int32, (PACK, 1), 0)
    place_row = lax.broadcasted_iota(jnp.int32, (1, PACK), 1)
    proj = dot(one_hot(place_col, perm_row[...]), proj, NN)
    proj_out[...] = proj.astype(BF16)
    offset, same = doc_places(doc_len)
    activated = []
    for kind in range(3):
        pre = conv_part(proj[:, 256 * kind : 256 * kind + 256], small, layer, kind, offset)
        activated.append(pre * sigmoid(pre))
    col = lax.broadcasted_iota(jnp.int32, (PACK, PACK), 0)
    row = lax.broadcasted_iota(jnp.int32, (PACK, PACK), 1)
    strict = same & (col > row)
    tri = same & (col >= row)
    heads = []
    for head in range(2):
        lanes = slice(128 * head, 128 * head + 128)
        query = halves(unit(activated[0][:, lanes])[0] * HD**-0.5)
        key = halves(unit(activated[1][:, lanes])[0])
        value = activated[2][:, lanes]
        strength = sigmoid(proj[:, 768 + head : 769 + head])
        system = jnp.where(strict, strength * dot3(key, key, NT), 0.0)
        solved = inverse(system)
        inv_out[head] = solved
        fresh = dot3(halves(solved), halves(strength * value), NN)
        u_out[head] = fresh
        scores = jnp.where(tri, dot3(query, key, NT), 0.0)
        produced = dot3(halves(scores), halves(fresh), NN)
        o_out[head] = produced
        scale = lax.rsqrt(jnp.mean(produced * produced, axis=-1, keepdims=True) + 1e-05)
        heads.append((produced * scale * small[layer, 2:3, 0:128]).astype(BF16))
    mixed = jnp.concatenate(heads, axis=1)
    attended = dot(one_hot(perm_col[...], place_row), mixed, NN).astype(BF16)
    att_out[...] = attended
    part[...] = dot(attended, w_o[...], NN).astype(BF16)


def mixer(rows, w_q, w_o, small, perm_row, perm_col, doc_len, layer):
    return pl.pallas_call(
        functools.partial(mixer_kernel, layer=layer),
        out_shape=[
            sds((PACK, D), BF16),
            sds((PACK, QW), BF16),
            sds((2, PACK, PACK), F32),
            sds((2, PACK, HD), F32),
            sds((2, PACK, HD), F32),
            sds((PACK, 256), BF16),
            sds((PACK, D), BF16),
        ],
        in_specs=[VMEM] * 6 + [SMEM],
        out_specs=[VMEM] * 7,
        compiler_params=pltpu.CompilerParams(vmem_limit_bytes=VMEM_BYTES),
        name="mixer",
    )(rows, w_q, w_o, small, perm_row, perm_col, doc_len)


def mixer_back_kernel(
    grad,
    w_q,
    w_o,
    small,
    perm_row,
    perm_col,
    doc_len,
    proj_ref,
    inv_ref,
    u_ref,
    o_ref,
    att,
    normed,
    part,
    dw_q,
    dw_o,
    dsmall,
    *,
    layer,
):
    grad_att = dot(grad[...], w_o[...], NT).astype(BF16)
    dw_o[...] = dot(att[...], grad[...], TN).astype(BF16)
    place_col = lax.broadcasted_iota(jnp.int32, (PACK, 1), 0)
    place_row = lax.broadcasted_iota(jnp.int32, (1, PACK), 1)
    grad_att = dot(one_hot(place_col, perm_row[...]), grad_att, NN)
    proj = proj_ref[...].astype(F32)
    offset, same = doc_places(doc_len)
    pres, gates = [], []
    for kind in range(3):
        pre = conv_part(proj[:, 256 * kind : 256 * kind + 256], small, layer, kind, offset)
        pres.append(pre)
        gates.append(sigmoid(pre))
    col = lax.broadcasted_iota(jnp.int32, (PACK, PACK), 0)
    row = lax.broadcasted_iota(jnp.int32, (PACK, PACK), 1)
    strict = same & (col > row)
    tri = same & (col >= row)
    gain = small[layer, 2:3, 0:128]
    gain_grad = jnp.zeros((1, HD), F32)
    grads = [[], [], []]
    logit_grads = []
    for head in range(2):
        lanes = slice(128 * head, 128 * head + 128)
        act_q, act_k, value = [(pre * gate)[:, lanes] for pre, gate in zip(pres, gates)]
        query_f, scale_q = unit(act_q)
        key_f, scale_k = unit(act_k)
        query, key = halves(query_f * HD**-0.5), halves(key_f)
        strength = sigmoid(proj[:, 768 + head : 769 + head])
        produced = o_ref[head]
        scale = lax.rsqrt(jnp.mean(produced * produced, axis=-1, keepdims=True) + 1e-05)
        given = grad_att[:, lanes]
        weighted = given * gain
        inner = jnp.mean(weighted * produced, axis=-1, keepdims=True)
        grad_o = halves(scale * weighted - produced * (scale * scale * scale) * inner)
        gain_grad = gain_grad + jnp.sum(given * produced * scale, axis=0, keepdims=True)
        fresh = halves(u_ref[head])
        gram = dot3(key, key, NT)
        scores = halves(jnp.where(tri, dot3(query, key, NT), 0.0))
        grad_scores = halves(jnp.where(tri, dot3(grad_o, fresh, NT), 0.0))
        grad_fresh = halves(dot3(scores, grad_o, TN))
        grad_source = dot3(halves(inv_ref[head]), grad_fresh, TN)
        grad_system = jnp.where(strict, -dot3(halves(grad_source), fresh, NT), 0.0)
        grad_gram = halves(strength * grad_system)
        grad_query = dot3(grad_scores, key, NN)
        grad_key = (
            dot3(grad_scores, query, TN) + dot3(grad_gram, key, NN) + dot3(grad_gram, key, TN)
        )
        grad_value = strength * grad_source
        grad_strength = jnp.sum(grad_source * value, axis=-1, keepdims=True) + jnp.sum(
            grad_system * gram, axis=-1, keepdims=True
        )
        logit_grads.append(grad_strength * strength * (1.0 - strength))
        grads[0].append(
            HD**-0.5
            * (
                scale_q * grad_query
                - act_q
                * (scale_q * scale_q * scale_q)
                * jnp.sum(act_q * grad_query, axis=-1, keepdims=True)
            )
        )
        grads[1].append(
            scale_k * grad_key
            - act_k
            * (scale_k * scale_k * scale_k)
            * jnp.sum(act_k * grad_key, axis=-1, keepdims=True)
        )
        grads[2].append(grad_value)
    dsmall[...] = jnp.zeros_like(dsmall)
    dsmall[2:3, 0:128] = gain_grad
    pieces = []
    for kind in range(3):
        pre, gate = pres[kind], gates[kind]
        grad_pre = jnp.concatenate(grads[kind], axis=1) * gate * (1.0 + pre * (1.0 - gate))
        series = proj[:, 256 * kind : 256 * kind + 256]
        total = grad_pre * conv_taps(small, layer, 0, kind)
        dsmall[4 + kind : 5 + kind, 0:256] = jnp.sum(grad_pre * series, axis=0, keepdims=True)
        for tap in range(1, 4):
            kept = jnp.where(offset >= tap, grad_pre, 0.0)
            total = total + shifted(kept, -tap) * conv_taps(small, layer, tap, kind)
            dsmall[4 + tap * 3 + kind : 5 + tap * 3 + kind, 0:256] = jnp.sum(
                kept * shifted(series, tap), axis=0, keepdims=True
            )
        pieces.append(total.astype(BF16))
    lane = lax.broadcasted_iota(jnp.int32, (1, 128), 1)
    pieces.append(
        jnp.where(lane == 0, logit_grads[0], jnp.where(lane == 1, logit_grads[1], 0.0)).astype(BF16)
    )
    grad_proj = jnp.concatenate(pieces, axis=1)
    grad_proj = dot(one_hot(perm_col[...], place_row), grad_proj, NN).astype(BF16)
    part[...] = dot(grad_proj, w_q[...], NT).astype(BF16)
    dw_q[...] = dot(normed[...], grad_proj, TN).astype(BF16)


def mixer_back(grad, w_q, w_o, small, perm_row, perm_col, doc_len, saved, layer):
    return pl.pallas_call(
        functools.partial(mixer_back_kernel, layer=layer),
        out_shape=[
            sds((PACK, D), BF16),
            sds((D, QW), BF16),
            sds((256, D), BF16),
            sds((16, D), F32),
        ],
        in_specs=[VMEM] * 6 + [SMEM] + [VMEM] * 6,
        out_specs=[VMEM] * 4,
        compiler_params=pltpu.CompilerParams(vmem_limit_bytes=VMEM_BYTES),
        name="mixer_back",
    )(grad, w_q, w_o, small, perm_row, perm_col, doc_len, *saved)


def ffn_kernel(normed, weights, part, gate_out, up_out, total):
    step = pl.program_id(0)
    gate = dot(normed[...], weights[0], NT)
    up = dot(normed[...], weights[1], NT)
    gate_out[...] = gate
    up_out[...] = up
    hidden = (gate * sigmoid(gate) * up).astype(BF16)
    term = dot(hidden, weights[2], NN)

    @pl.when(step == 0)
    def _():
        total[...] = term

    @pl.when(step > 0)
    def _():
        total[...] += term

    @pl.when(step == 2)
    def _():
        part[...] = total[...].astype(BF16)


def ffn(normed, weights):
    return pl.pallas_call(
        ffn_kernel,
        grid=(3,),
        out_shape=[sds((PACK, D), BF16), sds((PACK, 768), F32), sds((PACK, 768), F32)],
        in_specs=[
            pl.BlockSpec((PACK, D), lambda i: (0, 0)),
            pl.BlockSpec((3, 256, D), lambda i: (0, i, 0)),
        ],
        out_specs=[
            pl.BlockSpec((PACK, D), lambda i: (0, 0)),
            pl.BlockSpec((PACK, 256), lambda i: (0, i)),
            pl.BlockSpec((PACK, 256), lambda i: (0, i)),
        ],
        scratch_shapes=[pltpu.VMEM((PACK, D), F32)],
        compiler_params=pltpu.CompilerParams(vmem_limit_bytes=VMEM_BYTES),
        name="ffn",
    )(normed, weights)


def ffn_back_kernel(grad, normed, weights, gate_ref, up_ref, part, dweights, total):
    step = pl.program_id(0)
    gate, up = gate_ref[...], up_ref[...]
    sig = sigmoid(gate)
    grad_hidden = dot(grad[...], weights[2], NT)
    grad_gate = (grad_hidden * up * sig * (1.0 + gate * (1.0 - sig))).astype(BF16)
    grad_up = (grad_hidden * gate * sig).astype(BF16)
    hidden = (gate * sig * up).astype(BF16)
    term = dot(grad_gate, weights[0], NN) + dot(grad_up, weights[1], NN)

    @pl.when(step == 0)
    def _():
        total[...] = term

    @pl.when(step > 0)
    def _():
        total[...] += term

    @pl.when(step == 2)
    def _():
        part[...] = total[...].astype(BF16)

    dweights[0] = dot(grad_gate, normed[...], TN).astype(BF16)
    dweights[1] = dot(grad_up, normed[...], TN).astype(BF16)
    dweights[2] = dot(hidden, grad[...], TN).astype(BF16)


def ffn_back(grad, normed, weights, gate, up):
    return pl.pallas_call(
        ffn_back_kernel,
        grid=(3,),
        out_shape=[sds((PACK, D), BF16), sds((3, 768, D), BF16)],
        in_specs=[
            pl.BlockSpec((PACK, D), lambda i: (0, 0)),
            pl.BlockSpec((PACK, D), lambda i: (0, 0)),
            pl.BlockSpec((3, 256, D), lambda i: (0, i, 0)),
            pl.BlockSpec((PACK, 256), lambda i: (0, i)),
            pl.BlockSpec((PACK, 256), lambda i: (0, i)),
        ],
        out_specs=[
            pl.BlockSpec((PACK, D), lambda i: (0, 0)),
            pl.BlockSpec((3, 256, D), lambda i: (0, i, 0)),
        ],
        scratch_shapes=[pltpu.VMEM((PACK, D), F32)],
        compiler_params=pltpu.CompilerParams(vmem_limit_bytes=VMEM_BYTES),
        name="ffn_back",
    )(grad, normed, weights, gate, up)


def collect_kernel(
    rows_ref,
    small_ref,
    q0_ref,
    q1_ref,
    f0_ref,
    f1_ref,
    o0_ref,
    o1_ref,
    rows_out,
    small_out,
    q_out,
    f_out,
    o_out,
    q_sum,
    f_sum,
    o_sum,
    q_in,
    f_in,
    o_in,
    g_near,
    g_left,
    g_right,
    d_near,
    d_left,
    d_right,
    q_near,
    q_left,
    q_right,
    o_near,
    o_left,
    o_right,
    o_far,
    small_sum,
    small_in,
    send,
    recv,
    pair_send,
    pair_recv,
    local,
    small_send,
    small_recv,
    o_send,
    o_recv,
):
    core, seq, z, y = place()
    partner = {"section": 1 - core}
    greet(
        [along_x(seq, k) for k in (1, 2, 3)]
        + [along_y(z, y, k) for k in (1, 2, 3)]
        + [along_z(z, y, k) for k in (1, 2, 3)]
        + [partner]
    )

    kept = []

    def pair(index, source, target):
        return remote(source, target, pair_send.at[index], pair_recv.at[index], partner)

    pair_small = pair(0, small_ref.at[1 - core], small_in.at[0])
    pair_small.start()
    layers = [
        (1, q0_ref, q1_ref, q_in, q_sum),
        (2, f0_ref, f1_ref, f_in, f_sum),
        (3, o0_ref, o1_ref, o_in, o_sum),
    ]
    keep = [pltpu.make_async_copy(rows_ref, rows_out.at[:, core], local.at[0])]
    pair_rows = pair(4, rows_ref, rows_out.at[:, core])
    for mine in (0, 1):

        @pl.when(core == mine)
        def _():
            for index, first, second, landing, total in layers:
                pair(index, (second, first)[mine], landing).start()
                pltpu.make_async_copy((first, second)[mine], total, local.at[index]).start()

    pair_rows.start()
    for copy in keep:
        copy.start()
    for index, first, second, landing, total in layers:
        pltpu.make_async_copy(first, total, local.at[index]).wait()
        pair(index, first, landing).wait()
        add_into(total, [landing])

    def half_rows(half):
        return pl.ds(32 * half, 32)

    def half_units(half):
        return pl.ds(32 * half, 32 - 16 * half)

    def half_planes(half):
        return pl.ds(2 * half, 2)

    def y_ring(sem, *refs):
        return RingReduce(
            y, along_y(z, y, 1), along_y(z, y, 3), *refs, send.at[sem], recv.at[sem]
        )

    def z_ring(sem, *refs):
        return RingReduce(
            z, along_z(z, y, 1), along_z(z, y, 3), *refs, send.at[sem], recv.at[sem]
        )

    g_one = z_ring(
        0,
        lambda index, half: f_sum.at[half, index],
        lambda half: g_near.at[half, pl.ds(0, 4)],
        lambda half: g_left.at[half, pl.ds(0, 4)],
        lambda half: g_right.at[half, pl.ds(0, 4)],
    )
    d_one = y_ring(
        1,
        lambda index, half: f_sum.at[2, half_planes(half), index],
        lambda half: d_near.at[half_planes(half)],
        lambda half: d_left.at[half_planes(half)],
        lambda half: d_right.at[half_planes(half)],
    )
    q_one = y_ring(
        2,
        lambda index, half: q_sum.at[half_planes(half), index],
        lambda half: q_near.at[half_planes(half)],
        lambda half: q_left.at[half_planes(half)],
        lambda half: q_right.at[half_planes(half)],
    )
    o_one = y_ring(
        3,
        lambda index, half: o_sum.at[index, half_rows(half)],
        lambda half: o_near.at[half_rows(half)],
        lambda half: o_left.at[half_rows(half)],
        lambda half: o_right.at[half_rows(half)],
    )
    g_two = y_ring(
        4,
        lambda index, half: f_sum.at[half, z, index],
        lambda half: g_near.at[half, 4],
        lambda half: g_left.at[half, 4],
        lambda half: g_right.at[half, 4],
    )
    d_two = z_ring(
        5,
        lambda index, half: f_sum.at[2, index, y, half_units(half)],
        lambda half: d_near.at[4, half_units(half)],
        lambda half: d_left.at[4, half_units(half)],
        lambda half: d_right.at[4, half_units(half)],
    )
    q_two = z_ring(
        6,
        lambda index, half: q_sum.at[index, y, half_rows(half)],
        lambda half: q_near.at[4, half_rows(half)],
        lambda half: q_left.at[4, half_rows(half)],
        lambda half: q_right.at[4, half_rows(half)],
    )
    first = [q_one, g_one, d_one, o_one]
    for ring in first:
        ring.start()

    pair_small.wait()
    small_sum[0] = small_ref[core] + small_in[0]
    stage = 0
    small_copies = []
    for axis in (along_y, along_z):
        copies = [
            remote(
                small_sum.at[stage],
                small_in.at[1 + 3 * stage + k],
                small_send.at[3 * stage + k],
                small_recv.at[3 * stage + k],
                axis(z, y, k + 1),
            )
            for k in range(3)
        ]
        for copy in copies:
            copy.start()
        small_copies += copies
        if stage == 0:
            for ring in first:
                ring.middle()
        for copy in copies:
            copy.wait_recv()
        small_sum[stage + 1] = (
            small_sum[stage]
            + small_in[1 + 3 * stage]
            + small_in[2 + 3 * stage]
            + small_in[3 + 3 * stage]
        )
        stage += 1
    small_out[seq] = small_sum[2]
    copies = [
        remote(
            small_sum.at[2],
            small_out.at[seq],
            small_send.at[6 + k],
            small_recv.at[6 + k],
            along_x(seq, k + 1),
        )
        for k in range(3)
    ]
    for copy in copies:
        copy.start()
    small_copies += copies

    for ring, follower in ((q_one, q_two), (g_one, g_two), (d_one, d_two), (o_one, None)):
        ring.arrive()
        ring.total()
        if follower is not None:
            follower.start()

    o_total = o_sum.at[y]
    o_copies = [
        remote(o_total, o_far.at[k], o_send.at[k], o_recv.at[k], along_z(z, y, 3 - k))
        for k in range(3)
    ]
    for k in range(3):

        @pl.when(lax.rem(z + 3 - k, 4) == seq)
        def _():
            o_copies[k].start()

    second = [q_two, g_two, d_two]
    for ring in second:
        ring.middle()
    for ring in second:
        ring.arrive()
        ring.total()

    def x_gather(sem, source, slot):
        return RingGather(
            seq, along_x(seq, 1), along_x(seq, 3), source, slot, send.at[sem], recv.at[sem]
        )

    third = [
        x_gather(
            7,
            lambda half: q_sum.at[z, y, half_rows(half)],
            lambda index, half: q_out.at[index, half_rows(half)],
        ),
        x_gather(
            8,
            lambda half: f_sum.at[half, z, y],
            lambda index, half: f_out.at[index, half],
        ),
        x_gather(
            9,
            lambda half: f_sum.at[2, z, y, half_units(half)],
            lambda index, half: f_out.at[index, 2, half_units(half)],
        ),
    ]
    for ring in third:
        ring.start()
    q_out[seq] = q_sum[z, y]
    f_out[seq] = f_sum[:, z, y]

    x_copies = [
        remote(o_out, o_out, o_send.at[3 + k], o_recv.at[3], along_x(seq, k + 1)) for k in range(3)
    ]

    @pl.when(z == seq)
    def _():
        for k in range(3):
            o_copies[k].wait_recv()
        o_out[...] = (
            o_sum[y].astype(F32)
            + o_far[0].astype(F32)
            + o_far[1].astype(F32)
            + o_far[2].astype(F32)
        ).astype(BF16)
        for copy in x_copies:
            copy.start()

    for ring in third:
        ring.middle()

    @pl.when(z == seq)
    def _():
        for copy in x_copies:
            copy.wait_send()

    @pl.when(z != seq)
    def _():
        x_copies[0].wait_recv()

    for k in range(3):

        @pl.when(lax.rem(z + 3 - k, 4) == seq)
        def _():
            o_copies[k].wait_send()

    for ring in third:
        ring.near()
        ring.far()
    for ring in first + second + third:
        ring.finish()
    for copy in copies:
        copy.wait_recv()
    for copy in small_copies:
        copy.wait_send()
    pair_rows.wait()
    for copy in keep:
        copy.wait()


def collect(rows, small, q, f, o):
    operands = (rows, small, *q, *f, *o)
    return pl.pallas_call(
        collect_kernel,
        out_shape=[
            sds((2, 2, ROWS, D), BF16),
            sds((4, 16, D), F32),
            sds((4, 64, QW), BF16),
            sds((4, 3, UNIT, D), BF16),
            sds((64, D), BF16),
        ],
        in_specs=[VMEM] * len(operands),
        out_specs=[VMEM] * 5,
        scratch_shapes=[
            pltpu.VMEM((4, 4, 64, QW), BF16),
            pltpu.VMEM((3, 4, 4, UNIT, D), BF16),
            pltpu.VMEM((4, 64, D), BF16),
            pltpu.VMEM((4, 4, 64, QW), BF16),
            pltpu.VMEM((3, 4, 4, UNIT, D), BF16),
            pltpu.VMEM((4, 64, D), BF16),
            pltpu.VMEM((2, 5, UNIT, D), BF16),
            pltpu.VMEM((2, 5, UNIT, D), BF16),
            pltpu.VMEM((2, 5, UNIT, D), BF16),
            pltpu.VMEM((5, UNIT, D), BF16),
            pltpu.VMEM((5, UNIT, D), BF16),
            pltpu.VMEM((5, UNIT, D), BF16),
            pltpu.VMEM((5, 64, QW), BF16),
            pltpu.VMEM((5, 64, QW), BF16),
            pltpu.VMEM((5, 64, QW), BF16),
            pltpu.VMEM((64, D), BF16),
            pltpu.VMEM((64, D), BF16),
            pltpu.VMEM((64, D), BF16),
            pltpu.VMEM((3, 64, D), BF16),
            pltpu.VMEM((3, 16, D), F32),
            pltpu.VMEM((7, 16, D), F32),
            pltpu.SemaphoreType.DMA((10, 6)),
            pltpu.SemaphoreType.DMA((10, 6)),
            pltpu.SemaphoreType.DMA((5,)),
            pltpu.SemaphoreType.DMA((5,)),
            pltpu.SemaphoreType.DMA((4,)),
            pltpu.SemaphoreType.DMA((9,)),
            pltpu.SemaphoreType.DMA((9,)),
            pltpu.SemaphoreType.DMA((6,)),
            pltpu.SemaphoreType.DMA((4,)),
        ],
        compiler_params=pltpu.CompilerParams(
            collective_id=2, has_side_effects=True, vmem_limit_bytes=VMEM_BYTES
        ),
        name="collect",
    )(*operands)


def local(
    block_in,
    cotangent,
    perm_rows,
    doc_lengths,
    norm_in,
    w_qkv,
    w_beta,
    conv_w,
    norm_head,
    w_out,
    norm_ffn,
    w_ffn,
    w_down,
):
    core, seq = lax.axis_index("section"), lax.axis_index("seq")

    def mine(array):
        return lax.dynamic_index_in_dim(array, core, 0, keepdims=False)[0]

    x, cot = mine(block_in), mine(cotangent)
    perm, doc_len = mine(perm_rows), mine(doc_lengths)
    perm_row, perm_col = perm[None, :], perm[:, None]
    heads = lax.dynamic_slice_in_dim(conv_w[0], seq * 256, 256, 2).reshape(12, 256)
    small = jnp.concatenate(
        [
            norm_in,
            norm_ffn,
            jnp.pad(norm_head, ((0, 1), (0, D - HD))),
            jnp.pad(heads, ((0, 0), (0, D - 256))),
        ],
        axis=0,
    )
    q = jnp.concatenate(
        [
            lax.dynamic_slice_in_dim(w_qkv[0].reshape(64, 3, D), seq * 256, 256, 2).reshape(64, 768),
            jnp.pad(lax.dynamic_slice_in_dim(w_beta[0], seq * 2, 2, 1), ((0, 0), (0, 126))),
        ],
        axis=1,
    )
    units = jnp.concatenate([jnp.swapaxes(w_ffn[0], 1, 2), w_down], axis=0)
    units = jnp.pad(units, ((0, 0), (0, 16), (0, 0)))
    units = lax.dynamic_slice_in_dim(units, seq * UNIT, UNIT, 1)
    x_all, cot_all, small_all, q_all, f_all, o_all = spread(x, cot, small, q, units, w_out[0])
    q_all = q_all.reshape(2, D, QW)
    f_all = f_all.reshape(2, 3, 768, D)
    o_all = o_all.reshape(2, 256, D)

    rows_in, residuals, normed_ffn, gates, ups, saved = [x_all], [], [], [], [], []
    block_row = None
    for layer in (0, 1):
        part, *kept = mixer(
            rows_in[layer].reshape(PACK, D),
            q_all[layer],
            o_all[layer],
            small_all,
            perm_row,
            perm_col,
            doc_len,
            layer,
        )
        saved.append(kept)
        residual, gathered = seq_call(
            functools.partial(attended_kernel, layer=layer),
            [sds((ROWS, D), F32), sds((4, ROWS, D), BF16)],
            3 + layer,
            "attended",
            part.reshape(4, ROWS, D),
            rows_in[layer],
            small_all,
        )
        residuals.append(residual)
        normed_ffn.append(gathered.reshape(PACK, D))
        part, gate, up = ffn(normed_ffn[layer], f_all[layer])
        gates.append(gate)
        ups.append(up)
        if layer == 0:
            (gathered,) = seq_call(
                output_kernel,
                [sds((4, ROWS, D), BF16)],
                5,
                "output",
                part.reshape(4, ROWS, D),
                residual,
            )
            rows_in.append(gathered)
        else:
            (block_row,) = seq_call(
                last_output_kernel,
                [sds((ROWS, D), BF16)],
                6,
                "last_output",
                part.reshape(4, ROWS, D),
                residual,
            )

    outer = cot_all
    dq, df, do, dsmall = [None] * 2, [None] * 2, [None] * 2, [None] * 2
    for layer in (1, 0):
        part, df[layer] = ffn_back(
            outer.reshape(PACK, D), normed_ffn[layer], f_all[layer], gates[layer], ups[layer]
        )
        grad, gathered, gain_ffn = seq_call(
            functools.partial(back_ffn_kernel, layer=layer),
            [sds((ROWS, D), F32), sds((4, ROWS, D), BF16), sds((1, D), F32)],
            7 + layer,
            "back_ffn",
            part.reshape(4, ROWS, D),
            outer,
            residuals[layer],
            small_all,
        )
        part, dq[layer], do[layer], grad_small = mixer_back(
            gathered.reshape(PACK, D),
            q_all[layer],
            o_all[layer],
            small_all,
            perm_row,
            perm_col,
            doc_len,
            saved[layer],
            layer,
        )
        outer, gain_in = seq_call(
            functools.partial(back_in_kernel, layer=layer, last=layer == 0),
            [sds((4, ROWS, D) if layer else (ROWS, D), BF16), sds((1, D), F32)],
            9 + layer,
            "back_in",
            part.reshape(4, ROWS, D),
            grad,
            rows_in[layer],
            small_all,
        )
        dsmall[layer] = jnp.concatenate([gain_in, gain_ffn, grad_small[2:]], axis=0)

    rows, small_sum, q_sum, f_sum, o_sum = collect(
        jnp.stack([block_row, outer]),
        jnp.stack(dsmall),
        [d.reshape(4, 4, 64, QW) for d in dq],
        [d.reshape(3, 4, 4, UNIT, D) for d in df],
        [d.reshape(4, 64, D) for d in do],
    )
    total = jnp.sum(small_sum, axis=0)
    grad_conv = jnp.transpose(small_sum[:, 4:, :256].reshape(4, 4, 3, 256), (1, 2, 0, 3))
    grad_qkv = jnp.transpose(q_sum[:, :, :768].reshape(4, 64, 3, 256), (1, 2, 0, 3))
    grad_beta = jnp.transpose(q_sum[:, :, 768:770], (1, 0, 2))
    grad_units = jnp.swapaxes(f_sum, 0, 1).reshape(3, 192, D)[:, :176].astype(F32)
    return (
        rows[0][:, None],
        rows[1][:, None],
        total[0:1],
        grad_qkv.reshape(1, 64, 3 * D).astype(F32),
        grad_beta.reshape(1, 64, H).astype(F32),
        grad_conv.reshape(1, 4, 3, D),
        total[2:3, :HD],
        o_sum[None].astype(F32),
        total[1:2],
        jnp.swapaxes(grad_units[:2], 1, 2)[None],
        grad_units[2][None],
    )


def solution(mesh):
    placed = (
        P(None, "fsdp", "seq", None),
        P(None, "fsdp", "seq", None),
        P(None, "fsdp", None),
        P(None, "fsdp", None),
        P("section", None),
        P("section", "fsdp", None),
        P("section", "fsdp", None),
        P("section", None, None, None),
        P("section", None),
        P("section", "fsdp", None),
        P("section", None),
        P("section", None, None, "fsdp"),
        P("section", "fsdp", None),
    )
    return jax.shard_map(
        local,
        mesh=mesh,
        in_specs=placed,
        out_specs=(
            P(None, "fsdp", "seq", None),
            P(None, "fsdp", "seq", None),
            P("section", None),
            P("section", "fsdp", None),
            P("section", "fsdp", None),
            P("section", None, None, None),
            P("section", None),
            P("section", "fsdp", None),
            P("section", None),
            P("section", None, None, "fsdp"),
            P("section", "fsdp", None),
        ),
        check_vma=False,
    )
```

time: 1810 us -> 428 us (0.24)
  the two profiles are of different devices: /device:TPU:0 before, /device:TPU:2 now
where the time goes in v1:
time: 428 us; the launch traced here: 419 us
  Pallas kernels  378 us (88%)
  local copies, waits for them, and re-layouts  31.2 us (7%)
  other arithmetic  8.84 us (2%)
    pallas_call x8, Pallas kernels, seq_call(): pl.pallas_call(kernel, out_shape=out_shape, in_specs=[VMEM] * len(operand...  139 us
    pallas_call x1, Pallas kernels, collect(): pl.pallas_call(collect_kernel, out_shape=[sds((2, 2, ROWS, D), BF16), sds...  93 us
    pallas_call x1, Pallas kernels, spread(): pl.pallas_call(spread_kernel, out_shape=[sds((4, ROWS, D), BF16), sds((4,...  66.1 us
    pallas_call x2, Pallas kernels, mixer(): pl.pallas_call(functools.partial(mixer_kernel, layer=layer), out_shape=[s...  30.5 us
    pallas_call x2, Pallas kernels, mixer_back(): pl.pallas_call(functools.partial(mixer_back_kernel, layer=layer), out_sha...  20.1 us
    pallas_call x2, Pallas kernels, ffn_back(): pl.pallas_call(ffn_back_kernel, grid=(3,), out_shape=[sds((PACK, D), BF16...  17.7 us
    pallas_call x2, Pallas kernels, ffn(): pl.pallas_call(ffn_kernel, grid=(3,), out_shape=[sds((PACK, D), BF16), sd...  11.8 us
    slice x1, local copies, waits for them, and re-layouts, local(): part, gate, up = ffn(normed_ffn[layer], f_all[layer])  9.54 us

profile of v1, /device:TPU:2, one launch (start us, length us, event | category | flops | bytes accessed | tf_op | source)
XLA Modules:
  0.0 419.4 jit_solution(15207407075576030188)
XLA Ops:
  0.7 0.7 fusion.6
  1.4 1.2 fusion.7.doc_len
  2.6 1.2 fusion.8
  3.9 0.1 copy.43
  4.0 1.4 select_maximum_fusion.small_ref
  5.3 0.8 copy.44.perm_col
  6.1 1.7 dynamic-slice_bitcast_fusion
  7.8 1.8 fusion.2.f_ref
  9.6 0.6 reshape_squeeze.3
  10.3 0.7 fusion.4.q_ref
  10.9 66.1 %spread.1 = (bf16[4,64,1024]{2,1,0:T(8,128)(2,1)}, bf16[4,64,1024]{2,1,0:T(8,128)(2,1)}, f32[2,16,1024]{2,1,0:T(8,128)}, bf16[2,4,4,64,896]{4,3,2,1,0:T(8,128)(2...) custom-call(bf16[64,1024]{1,0:T(8,128)(2,1)} %get-tuple-element.171.x_ref, ...), custom_call_target="tpu_custom_call" | custom-call | tf_op jit(solution)/shard_map/spread/pallas_call | solution.py:390
  77.0 4.3 %fusion.11 = (bf16[1,4,4,64,896]{4,3,2,1,0:T(8,128)(2,1)}, bf16[1,4,4,64,896]{4,3,2,1,0:T(8,128)(2,1)}) fusion(bf16[2,4,4,64,896]{4,3,2,1,0:T(8,128)(2,1)} %get-tuple-element.69), kind=kLoop, calls=%fused_computation.38 | loop fusion | bytes 7340032 | tf_op jit(solution)/shard_map/slice | solution.py:1301
  81.4 1.0 fusion.12
  82.4 15.2 %mixer.2 = (bf16[256,1024]{1,0:T(8,128)(2,1)}, bf16[256,896]{1,0:T(8,128)(2,1)}, f32[2,256,256]{2,1,0:T(8,128)}, f32[2,256,128]{2,1,0:T(8,128)}, f32[2,256,128]{...) custom-call(bf16[256,1024]{1,0:T(8,128)(2,1)} %bitcast.93, bf16[1024,896]{1,0:T(8,128)(2,1)} %bitcast.82, ...), custom_call_target="tpu_custom_call" | custom-call | tf_op jit(solution)/shard_map/mixer/pallas_call | solution.py:656
  97.6 20.2 %attended.2 = (f32[64,1024]{1,0:T(8,128)}, bf16[4,64,1024]{2,1,0:T(8,128)(2,1)}) custom-call(bf16[4,64,1024]{2,1,0:T(8,128)(2,1)} %bitcast.112, bf16[4,64,1024]{2,1,0:T(8,128)(2,1)} %get-tuple-element.68.rows, f32[2,16,1024]{2,1,0:T(8,128)} %get-tuple-element.71.small), custom_call_target="tpu_custom_call" | custom-call | tf_op jit(solution)/shard_map/attended/pallas_call | solution.py:532
  117.9 9.5 %fusion.10 = (bf16[1,3,4,4,48,1024]{5,4,3,2,1,0:T(8,128)(2,1)}, bf16[1,3,4,4,48,1024]{5,4,3,2,1,0:T(8,128)(2,1)}) fusion(bf16[2,3,4,4,48,1024]{5,4,3,2,1,0:T(8,128)(2,1)} %get-tuple-element.74), kind=kLoop, calls=%fused_computation.37 | loop fusion | bytes 18874368 | tf_op jit(solution)/shard_map/slice | solution.py:1321
  127.4 5.7 %ffn.2 = (bf16[256,1024]{1,0:T(8,128)(2,1)}, f32[256,768]{1,0:T(8,128)}, f32[256,768]{1,0:T(8,128)}) custom-call(bf16[256,1024]{1,0:T(8,128)(2,1)} %bitcast.96, bf16[3,768,1024]{2,1,0:T(8,128)(2,1)} %bitcast.78), custom_call_target="tpu_custom_call" | custom-call | tf_op jit(solution)/shard_map/ffn/pallas_call | solution.py:827
  133.1 18.2 %output.1.rows = bf16[4,64,1024]{2,1,0:T(8,128)(2,1)} custom-call(bf16[4,64,1024]{2,1,0:T(8,128)(2,1)} %bitcast.114, f32[64,1024]{1,0:T(8,128)} %get-tuple-element.76.residual), custom_call_target="tpu_custom_call" | custom-call | tf_op jit(solution)/shard_map/output/pallas_call | solution.py:532
  151.4 15.3 %mixer.3 = (bf16[256,1024]{1,0:T(8,128)(2,1)}, bf16[256,896]{1,0:T(8,128)(2,1)}, f32[2,256,256]{2,1,0:T(8,128)}, f32[2,256,128]{2,1,0:T(8,128)}, f32[2,256,128]{...) custom-call(bf16[256,1024]{1,0:T(8,128)(2,1)} %bitcast.86, bf16[1024,896]{1,0:T(8,128)(2,1)} %bitcast.84, ...), custom_call_target="tpu_custom_call" | custom-call | tf_op jit(solution)/shard_map/mixer/pallas_call | solution.py:656
  166.7 20.2 %attended.3 = (f32[64,1024]{1,0:T(8,128)}, bf16[4,64,1024]{2,1,0:T(8,128)(2,1)}) custom-call(bf16[4,64,1024]{2,1,0:T(8,128)(2,1)} %bitcast.113, bf16[4,64,1024]{2,1,0:T(8,128)(2,1)} %output.1.rows, f32[2,16,1024]{2,1,0:T(8,128)} %get-tuple-element.71.small), custom_call_target="tpu_custom_call" | custom-call | tf_op jit(solution)/shard_map/attended/pallas_call | solution.py:532
  186.9 6.1 %ffn.3 = (bf16[256,1024]{1,0:T(8,128)(2,1)}, f32[256,768]{1,0:T(8,128)}, f32[256,768]{1,0:T(8,128)}) custom-call(bf16[256,1024]{1,0:T(8,128)(2,1)} %bitcast.98, bf16[3,768,1024]{2,1,0:T(8,128)(2,1)} %bitcast.80), custom_call_target="tpu_custom_call" | custom-call | tf_op jit(solution)/shard_map/ffn/pallas_call | solution.py:827
  192.9 9.9 %last_output.1 = bf16[64,1024]{1,0:T(8,128)(2,1)} custom-call(bf16[4,64,1024]{2,1,0:T(8,128)(2,1)} %bitcast.110, f32[64,1024]{1,0:T(8,128)} %get-tuple-element.80.residual), custom_call_target="tpu_custom_call" | custom-call | tf_op jit(solution)/shard_map/last_output/pallas_call | solution.py:532
  202.8 8.8 %ffn_back.2 = (bf16[256,1024]{1,0:T(8,128)(2,1)}, bf16[3,768,1024]{2,1,0:T(8,128)(2,1)}) custom-call(bf16[256,1024]{1,0:T(8,128)(2,1)} %bitcast.100, bf16[256,1024]{1,0:T(8,128)(2,1)} %bitcast.99, bf16[3,768,1024]{2,1,0:T(8,128)(2,1)} %bitcast.81, f32[256,768]{1,0:T(8,128)} %get-tuple-element.82.gate_ref, f32[256,768]{1,0:T(8,128)} %get-tuple-element.83.up_ref), custom_call_target="tpu_custom_call" | custom-call | tf_op jit(solution)/shard_map/ffn_back/pallas_call | solution.py:874
  211.6 20.2 %back_ffn.2 = (f32[64,1024]{1,0:T(8,128)}, bf16[4,64,1024]{2,1,0:T(8,128)(2,1)}, f32[1,1024]{1,0:T(1,128)}) custom-call(bf16[4,64,1024]{2,1,0:T(8,128)(2,1)} %bitcast.118, bf16[4,64,1024]{2,1,0:T(8,128)(2,1)} %get-tuple-element.81.outer, f32[64,1024]{1,0:T(8,128)} %get-tuple-element.80.residual, f32[2,16,1024]{2,1,0:T(8,128)} %get-tuple-element.71.small), custom_call_target="tpu_custom_call" | custom-call | tf_op jit(solution)/shard_map/back_ffn/pallas_call | solution.py:532
  231.9 10.0 %mixer_back.2 = (bf16[256,1024]{1,0:T(8,128)(2,1)}, bf16[1024,896]{1,0:T(8,128)(2,1)}, bf16[256,1024]{1,0:T(8,128)(2,1)}, f32[16,1024]{1,0:T(8,128)}) custom-call(bf16[256,1024]{1,0:T(8,128)(2,1)} %bitcast.109, bf16[1024,896]{1,0:T(8,128)(2,1)} %bitcast.85, bf16[256,1024]{1,0:T(8,128)(2,1)} %bitcast.92, f32[2,16,1024]{2,1,0:T(8,128)} %get-tuple-element.71.small, ...), custom_call_target="tpu_custom_call" | custom-call | tf_op jit(solution)/shard_map/mixer_back/pallas_call | solution.py:789
  241.9 18.8 %back_in.2 = (bf16[4,64,1024]{2,1,0:T(8,128)(2,1)}, f32[1,1024]{1,0:T(1,128)}) custom-call(bf16[4,64,1024]{2,1,0:T(8,128)(2,1)} %bitcast.117, f32[64,1024]{1,0:T(8,128)} %get-tuple-element.93.grad_ref, bf16[4,64,1024]{2,1,0:T(8,128)(2,1)} %output.1.rows, f32[2,16,1024]{2,1,0:T(8,128)} %get-tuple-element.71.small), custom_call_target="tpu_custom_call" | custom-call | tf_op jit(solution)/shard_map/back_in/pallas_call | solution.py:532
  260.8 8.8 %ffn_back.3 = (bf16[256,1024]{1,0:T(8,128)(2,1)}, bf16[3,768,1024]{2,1,0:T(8,128)(2,1)}) custom-call(bf16[256,1024]{1,0:T(8,128)(2,1)} %bitcast.101, bf16[256,1024]{1,0:T(8,128)(2,1)} %bitcast.97, bf16[3,768,1024]{2,1,0:T(8,128)(2,1)} %bitcast.79, f32[256,768]{1,0:T(8,128)} %get-tuple-element.95.gate_ref, f32[256,768]{1,0:T(8,128)} %get-tuple-element.96.up_ref), custom_call_target="tpu_custom_call" | custom-call | tf_op jit(solution)/shard_map/ffn_back/pallas_call | solution.py:874
  269.6 21.0 %back_ffn.3 = (f32[64,1024]{1,0:T(8,128)}, bf16[4,64,1024]{2,1,0:T(8,128)(2,1)}, f32[1,1024]{1,0:T(1,128)}) custom-call(bf16[4,64,1024]{2,1,0:T(8,128)(2,1)} %bitcast.119, bf16[4,64,1024]{2,1,0:T(8,128)(2,1)} %get-tuple-element.94.outer, f32[64,1024]{1,0:T(8,128)} %get-tuple-element.76.residual, f32[2,16,1024]{2,1,0:T(8,128)} %get-tuple-element.71.small), custom_call_target="tpu_custom_call" | custom-call | tf_op jit(solution)/shard_map/back_ffn/pallas_call | solution.py:532
  290.6 10.1 %mixer_back.3 = (bf16[256,1024]{1,0:T(8,128)(2,1)}, bf16[1024,896]{1,0:T(8,128)(2,1)}, bf16[256,1024]{1,0:T(8,128)(2,1)}, f32[16,1024]{1,0:T(8,128)}) custom-call(bf16[256,1024]{1,0:T(8,128)(2,1)} %bitcast.108, bf16[1024,896]{1,0:T(8,128)(2,1)} %bitcast.83, bf16[256,1024]{1,0:T(8,128)(2,1)} %bitcast.90, f32[2,16,1024]{2,1,0:T(8,128)} %get-tuple-element.71.small, ...), custom_call_target="tpu_custom_call" | custom-call | tf_op jit(solution)/shard_map/mixer_back/pallas_call | solution.py:789
  300.7 10.2 %back_in.3 = (bf16[64,1024]{1,0:T(8,128)(2,1)}, f32[1,1024]{1,0:T(1,128)}) custom-call(bf16[4,64,1024]{2,1,0:T(8,128)(2,1)} %bitcast.116, f32[64,1024]{1,0:T(8,128)} %get-tuple-element.106.grad_ref, bf16[4,64,1024]{2,1,0:T(8,128)(2,1)} %get-tuple-element.68.rows, f32[2,16,1024]{2,1,0:T(8,128)} %get-tuple-element.71.small), custom_call_target="tpu_custom_call" | custom-call | tf_op jit(solution)/shard_map/back_in/pallas_call | solution.py:532
  310.9 1.6 pad_maximum_fusion.rows_ref
  312.6 0.7 maximum_bitcast_fusion
  313.4 0.7 pad_maximum_fusion.1.small_ref
  314.0 93.0 %collect.1 = (bf16[2,2,64,1024]{3,2,1,0:T(8,128)(2,1)}, f32[4,16,1024]{2,1,0:T(8,128)}, bf16[4,64,896]{2,1,0:T(8,128)(2,1)}, bf16[4,3,48,1024]{3,2,1,0:T(8,128)(2,1)}, bf16[64,1024]{1,0:T(8,128)(2,1)}) custom-call(bf16[2,64,1024]{2,1,0:T(8,128)(2,1)} %pad_maximum_fusion.rows_ref, f32[2,16,1024]{2,1,0:T(8,128)} %pad_maximum_fusion.1.small_ref, ...), custom_call_target="tpu_custom_call" | custom-call | tf_op jit(solution)/shard_map/collect/pallas_call | solution.py:1198
  407.1 1.9 slice_bitcast_fusion.1
  409.0 1.0 reduce_sum.9
  410.0 0.8 slice.82
  410.9 0.7 reshape.185
  411.5 0.5 slice.89
  412.0 0.6 fusion.13
  412.6 0.7 copy.49
  413.3 0.7 bitcast_convert_fusion
  414.1 0.4 reshape.190
  414.6 0.5 copy.48
  415.1 1.3 reshape.187
  416.5 0.2 slice_convert_fusion
  416.7 0.9 slice.93
  417.7 1.3 slice_bitcast_fusion
  (39 shorter events, 0.4 us)
Async XLA Ops:
  0.6 3.2 copy-start
  0.7 8.9 %copy-start.6 = (bf16[1,64,3072]{2,1,0:T(8,128)(2,1)S(1)}, bf16[1,64,3072]{2,1,0:T(8,128)(2,1)}, u32[]{:S(2)}) copy-start(bf16[1,64,3072]{2,1,0:T(8,128)(2,1)} %param.18) | copy-start | bytes 1179652
  77.0 4.4 %copy-start.3 = (bf16[2,4,64,1024]{3,2,1,0:T(8,128)(2,1)S(1)}, bf16[2,4,64,1024]{3,2,1,0:T(8,128)(2,1)}, u32[]{:S(2)}) copy-start(bf16[2,4,64,1024]{3,2,1,0:T(8,128)(2,1)} %get-tuple-element.70) | copy-start | bytes 3145732
  290.6 20.3 %copy-start.4 = (bf16[64,1024]{1,0:T(8,128)(2,1)S(1)}, bf16[64,1024]{1,0:T(8,128)(2,1)}, u32[]{:S(2)}) copy-start(bf16[64,1024]{1,0:T(8,128)(2,1)} %last_output.1) | copy-start | bytes 393220
  300.6 11.9 %copy-start.9 = (f32[16,1024]{1,0:T(8,128)S(1)}, f32[16,1024]{1,0:T(8,128)}, u32[]{:S(2)}) copy-start(f32[16,1024]{1,0:T(8,128)} %get-tuple-element.110) | copy-start | bytes 196612
  300.7 11.9 %copy-start.12 = (f32[1,1024]{1,0:T(1,128)S(1)}, f32[1,1024]{1,0:T(1,128)}, u32[]{:S(2)}) copy-start(f32[1,1024]{1,0:T(1,128)} %get-tuple-element.109) | copy-start | bytes 12292
  300.7 12.6 %copy-start.8 = (f32[16,1024]{1,0:T(8,128)S(1)}, f32[16,1024]{1,0:T(8,128)}, u32[]{:S(2)}) copy-start(f32[16,1024]{1,0:T(8,128)} %get-tuple-element.113) | copy-start | bytes 196612
  300.7 12.6 %copy-start.10 = (f32[1,1024]{1,0:T(1,128)S(1)}, f32[1,1024]{1,0:T(1,128)}, u32[]{:S(2)}) copy-start(f32[1,1024]{1,0:T(1,128)} %get-tuple-element.112) | copy-start | bytes 12292
  300.7 12.6 %copy-start.11 = (f32[1,1024]{1,0:T(1,128)S(1)}, f32[1,1024]{1,0:T(1,128)}, u32[]{:S(2)}) copy-start(f32[1,1024]{1,0:T(1,128)} %get-tuple-element.111) | copy-start | bytes 12292
  407.0 5.6 %copy-start.5 = (bf16[4,64,896]{2,1,0:T(8,128)(2,1)S(1)}, bf16[4,64,896]{2,1,0:T(8,128)(2,1)}, u32[]{:S(2)}) copy-start(bf16[4,64,896]{2,1,0:T(8,128)(2,1)} %get-tuple-element.122) | copy-start | bytes 1376260
  407.1 6.3 %copy-start.7 = (bf16[64,1024]{1,0:T(8,128)(2,1)S(1)}, bf16[64,1024]{1,0:T(8,128)(2,1)}, u32[]{:S(2)}) copy-start(bf16[64,1024]{1,0:T(8,128)(2,1)} %get-tuple-element.123) | copy-start | bytes 393220
  414.5 1.8 copy-start.2
  416.5 2.5 copy-start.1
